TPU v7x, 32 devices: a whole 2x2x4 slice. The times are simulated.
32 devices in a mesh: grp: 2 (over y), sta: 4 (over z), tm: 2 (over x), comp: 2 (over core).
Axes of the slice: x: 2, y: 2, z: 4, core: 2. Of those that a mesh axis runs over, the one named last changes fastest.
Arguments:
- data: bfloat16 [16, 3, 4096], P(('grp', 'sta'), None, 'tm'), parts along dimension 0, may hold values from -240 to 240
- templates: bfloat16 [16, 64, 3, 400], P(('grp', 'sta'), 'comp'), parts along dimension 0, may hold values from -6 to 6
- moveouts: int32 [16, 64], P(('grp', 'sta'), 'comp'), parts along dimension 0, may hold values from 0 to 624, as said below
- mask: int32 [16, 4], P(('grp', 'sta'), 'tm'), parts along dimension 0, may hold values from 0 to 1, as said below
Outputs:
- network: float32 [128, 4096], P(('grp', 'comp'), 'tm'), parts along dimension 0
There are 2 independent parts, one for each index of `grp`. A program takes and returns all parts, laid end to end along the dimension named above; each array names one. Nothing has to cross between parts.
Inputs may be any that keep to these rules, and one draw needn't show every extreme that they name: `moveouts`: for every template some station has shift 625 - 1 and some station has shift 0. `mask`: every availability block has at least one available station.
All inputs are finite; a program needn't handle non-finite values.
Results may differ from a plain program's by a relative error of at most 0.0003.
Values may be sent and summed in bfloat16 or wider, within the bound.
No kernel may reach another device: no remote copies, remote signals or barrier semaphores. Data moves between devices by JAX's collectives and lax.ppermute only.
A program may use at most 64 MiB of HBM per device.

v0:
```python
import math

import jax
import jax.numpy as jnp
from jax import lax
from jax.sharding import PartitionSpec as P

MOVE = 625


eps_energy = 1e-06
tap_group = 16


def shifted(value, axis, steps):
    count = lax.axis_size(axis)
    first, last = (max(0, -steps), min(count, count - steps))
    return lax.ppermute(value, axis, [(source, source + steps) for source in range(first, last)])


def shards(data, templates, moveouts, mask):
    samples = data.shape[2]
    length = templates.shape[3]
    trailing = length + MOVE - 1
    blocks = mask.shape[1]
    block_len = samples // blocks
    span = samples + MOVE
    groups = length // tap_group
    following = shifted(data[:, :, :trailing], "tm", -1)
    extended = jnp.concatenate([data, following], axis=2)
    template_scale = lax.rsqrt(
        jnp.einsum("stck,stck->st", templates, templates, preferred_element_type=jnp.float32)
        + eps_energy
    )
    offsets = jnp.arange(samples, dtype=jnp.int32)
    factor = math.sqrt(3.0 * length)
    flag_rows = mask.astype(jnp.float32)
    count_local = templates.shape[1]

    def one_station(running, inputs):
        waveform, bank, shifts, flags, scale_row = inputs

        def add_taps(index, carry):
            product_sum, energy_sum = carry
            first_tap = index * tap_group
            pieces = jnp.stack(
                [
                    lax.dynamic_slice_in_dim(waveform, first_tap + offset, span, 1)
                    for offset in range(tap_group)
                ],
                axis=1,
            )
            taps = lax.dynamic_slice_in_dim(bank, first_tap, tap_group, 2)
            product_sum = product_sum + jnp.einsum(
                "tcu,cup->tp", taps, pieces, preferred_element_type=jnp.float32
            )
            widened = pieces.astype(jnp.float32)
            energy_sum = energy_sum + jnp.sum(widened * widened, axis=(0, 1))
            return (product_sum, energy_sum)

        start = (jnp.zeros((count_local, span), jnp.float32), jnp.zeros((span,), jnp.float32))
        products, energy = lax.fori_loop(0, groups, add_taps, start)
        normalized = jnp.where(
            energy[None, :] > 0.0,
            products * scale_row[:, None] * lax.rsqrt(energy + eps_energy)[None, :],
            0.0,
        )
        aligned = jnp.take_along_axis(normalized, shifts[:, None] + offsets[None, :], axis=1)
        weight = jnp.repeat(flags, block_len)
        return (running + weight[None, :] * aligned, None)

    empty = jnp.zeros((count_local, samples), jnp.float32)
    running, _ = lax.scan(
        one_station, empty, (extended, templates, moveouts, flag_rows, template_scale)
    )
    live_counts = jnp.sum(flag_rows, axis=0)
    summed, total_counts = lax.psum((running, live_counts), "sta")
    count_row = jnp.repeat(total_counts, block_len)
    return summed * (factor * lax.rsqrt(count_row))[None, :]


def solution(mesh):
    placed = (
        P(("grp", "sta"), None, "tm"),
        P(("grp", "sta"), "comp", None, None),
        P(("grp", "sta"), "comp"),
        P(("grp", "sta"), "tm"),
    )
    return jax.shard_map(
        shards, mesh=mesh, in_specs=placed, out_specs=P(("grp", "comp"), "tm"), check_vma=False
    )
```

profile of v0, /device:TPU:0, one launch (start us, length us, event | category | flops | bytes accessed | tf_op | source)
XLA Modules:
  0.0 1222.7 jit_solution(17832408497834587988)
XLA Ops:
  6.5 0.8 copy.25
  7.4 1.3 collective-permute-start
  8.7 1.1 fusion.15
  9.7 0.7 convert_reduce_fusion
  10.4 14.0 %psum.15 = f32[2]{0:T(128)} all-reduce(f32[2]{0:T(128)S(1)} %convert_reduce_fusion), channel_id=1, replica_groups=mesh['grp'=2,'sta'=4,'tm'=2,'comp'=2] {'sta'}, use_global_device_ids=true, to_apply=%region_7.8 | all-reduce | flops 2 | bytes 16 | tf_op jit(solution)/shard_map/psum | solution.py:77
  24.4 0.7 convert_element_type.13
  25.2 1153.5 %while.45 = (s32[]{:T(128)}, f32[32,2048]{1,0:T(8,128)S(1)}, f32[2,2]{1,0:T(2,128)S(1)}, s32[2,32]{1,0:T(2,128)S(1)}, bf16[2,3,3072]{2,1,0:T(4,128)(2,1)S(1)}, /...) while((s32[]{:T(128)}, f32[32,2048]{1,0:T(8,128)S(1)}, ...), condition=%wide.region_4.5_spmd.clone.clone, body=%wide.region_0.4_spmd.clone.clone.sunk | while | flops 10342859 | bytes 7053338 | solution.py:73
  25.5 56.2 %while.46 = (s32[]{:T(128)}, f32[32,2673]{1,0:T(8,128)S(1)}, f32[2673]{0:T(1024)S(1)}, bf16[32,3,400]{0,2,1:T(8,128)(2,1)S(1)}, bf16[3,3072]{1,0:T(4,128)(2,1)S(...) while((s32[]{:T(128)}, f32[32,2673]{1,0:T(8,128)S(1)}, ...), condition=%wide.region_3.3_spmd.clone, body=%wide.region_1.2_spmd.clone.sunk | while | flops 8770182 | bytes 2796741 | solution.py:62
  26.6 0.8 stack.188
  28.8 0.8 stack.188
  31.1 0.8 stack.188
  33.3 0.8 stack.188
  35.6 0.8 stack.188
  37.8 0.8 stack.188
  40.0 0.8 stack.188
  42.3 0.8 stack.188
  44.5 0.8 stack.188
  46.8 0.8 stack.188
  49.0 0.8 stack.188
  51.3 0.8 stack.188
  53.5 0.8 stack.188
  55.8 0.8 stack.188
  58.0 0.8 stack.188
  60.3 0.8 stack.188
  62.5 0.8 stack.188
  64.8 0.8 stack.188
  67.0 0.8 stack.188
  69.3 0.8 stack.188
  71.5 0.8 stack.188
  73.8 0.8 stack.188
  76.0 0.8 stack.188
  78.3 0.8 stack.188
  80.5 0.8 stack.188
  82.1 519.5 %gather_fusion = f32[65536]{0:T(1024)S(1)} fusion(f32[32,2673]{1,0:T(8,128)S(1)} %multiply_select_fusion.2, s32[65536]{0:T(1024)S(1)} %bitcast.84), kind=kCustom, calls=%fused_computation.clone.clone.1 | custom fusion | bytes 1048576 | tf_op jit(solution)/shard_map/while/body/eval_jaxpr/jit(take_along_axis)/gather | solution.py:68
  602.2 56.2 %while.46 = (s32[]{:T(128)}, f32[32,2673]{1,0:T(8,128)S(1)}, f32[2673]{0:T(1024)S(1)}, bf16[32,3,400]{0,2,1:T(8,128)(2,1)S(1)}, bf16[3,3072]{1,0:T(4,128)(2,1)S(...) while((s32[]{:T(128)}, f32[32,2673]{1,0:T(8,128)S(1)}, ...), condition=%wide.region_3.3_spmd.clone, body=%wide.region_1.2_spmd.clone.sunk | while | flops 8770182 | bytes 2796741 | solution.py:62
  603.3 0.8 stack.188
  605.6 0.8 stack.188
  607.8 0.8 stack.188
  610.1 0.8 stack.188
  612.3 0.8 stack.188
  614.6 0.8 stack.188
  616.8 0.8 stack.188
  619.1 0.8 stack.188
  621.3 0.8 stack.188
  623.5 0.8 stack.188
  625.8 0.8 stack.188
  628.0 0.8 stack.188
  630.3 0.8 stack.188
  632.5 0.8 stack.188
  634.8 0.8 stack.188
  637.0 0.8 stack.188
  639.3 0.8 stack.188
  641.5 0.8 stack.188
  643.8 0.8 stack.188
  646.0 0.8 stack.188
  648.3 0.8 stack.188
  650.5 0.8 stack.188
  652.8 0.8 stack.188
  655.0 0.8 stack.188
  657.3 0.8 stack.188
  658.8 519.5 %gather_fusion = f32[65536]{0:T(1024)S(1)} fusion(f32[32,2673]{1,0:T(8,128)S(1)} %multiply_select_fusion.2, s32[65536]{0:T(1024)S(1)} %bitcast.84), kind=kCustom, calls=%fused_computation.clone.clone.1 | custom fusion | bytes 1048576 | tf_op jit(solution)/shard_map/while/body/eval_jaxpr/jit(take_along_axis)/gather | solution.py:68
  1178.7 0.7 copy-done
  1179.5 34.7 %all-reduce.2.cloned.1.call-done = f32[32,2048]{1,0:T(8,128)} async-done(((f32[32,2048]{1,0:T(8,128)}), f32[32,2048]{1,0:T(8,128)}) %all-reduce.2.cloned.1.call-update) | async-done | bytes 262160 | tf_op jit(solution)/shard_map/psum | solution.py:77
  1214.2 1.7 broadcast_multiply_fusion
  (1051 shorter events, 62.0 us)
Async XLA Ops:
  6.5 18.6 %copy-start.1 = (bf16[2,32,3,400]{3,1,2,0:T(8,128)(2,1)S(1)}, bf16[2,32,3,400]{3,1,2,0:T(8,128)(2,1)}, u32[]{:S(2)}) copy-start(bf16[2,32,3,400]{3,1,2,0:T(8,128)(2,1)} %param.9) | copy-start | bytes 460804
  6.5 18.6 %copy-start.2 = (s32[2,32]{1,0:T(2,128)S(1)}, s32[2,32]{1,0:T(2,128)}, u32[]{:S(2)}) copy-start(s32[2,32]{1,0:T(2,128)} %param.10) | copy-start | bytes 772
  6.5 1207.7 %all-reduce.2.cloned.1.call-start = ((), (), s32[]{:S(2)}) async-start(), calls=%async_computation | async-start | bytes 524288 | tf_op jit(solution)/shard_map/psum | solution.py:77
  7.4 17.8 %collective-permute-start = (bf16[2,3,1024]{2,1,0:T(4,128)(2,1)S(1)}, bf16[2,3,1024]{2,1,0:T(4,128)(2,1)S(1)}, u32[]{:S(2)}, u32[]{:S(2)}) collective-permute-start(bf16[2,3,1024]{2,1,0:T(4,128)(2,1)S(1)} %slice.6), channel_id=1, source_target_pairs={{2,0},{3,1},{6,4},{7,5},{10,8},{11,9},{14,12},{15,13},{18,16},{19,... | collective-permute-start | bytes 36872 | tf_op jit(solution)/shard_map/ppermute | solution.py:18
  25.2 1154.3 %copy-start.3 = (f32[2]{0:T(128)S(1)}, f32[2]{0:T(128)}, u32[]{:S(2)}) copy-start(f32[2]{0:T(128)} %psum.15) | copy-start | bytes 28
  1178.7 0.7 copy-start
Sparse Core Ops, SparseCore 0:
  1179.6 34.6 all-reduce.1
where the time goes:
time: 1220 us
  local copies, waits for them, and re-layouts  1120 us (92%)
  waiting for transfers between devices  34.7 us (3%)
  loops' own time  14.1 us (1%)
  blocking collectives  14 us (1%)
  between operations  13.5 us (1%)
  matrix products  12.9 us (1%)
    gather x4, local copies, waits for them, and re-layouts, one_station(): jnp.take_along_axis(normalized, shifts[:, None] + offsets[None, :], axis=1)  1040 us
    another operation x900, local copies, waits for them, and re-layouts, add_taps(): jnp.stack([lax.dynamic_slice_in_dim(waveform, first_tap + offset, span, 1...  81.7 us
    psum x1, waiting for transfers between devices, shards(): summed, total_counts = lax.psum((running, live_counts), 'sta')  34.7 us
  transfers between devices with their start and end apart: 2, of which 1 were waited for; matrix products, arithmetic and copies ran while one was open for 0% of the time, Pallas kernels for 0%

commit v1 on v0

v1 whole, which is shorter than its diff:
```python
import functools
import math

import jax
import jax.numpy as jnp
from jax import lax
from jax.experimental import pallas as pl
from jax.experimental.pallas import tpu as pltpu
from jax.sharding import PartitionSpec as P

MOVE = 625

eps_energy = 1e-06
LANES = 128
WIRE_SCALE = 2.0**13


def shifted(value, axis, steps):
    count = lax.axis_size(axis)
    first, last = (max(0, -steps), min(count, count - steps))
    return lax.ppermute(value, axis, [(source, source + steps) for source in range(first, last)])


def correlate(moves, flags, wave_ref, bank_ref, out_ref, hankel, aligned, sums, *, sizes):
    stations, comps, taps, count, samples, block_len = sizes
    width = wave_ref.shape[2]
    whole = taps // LANES
    tail = taps - whole * LANES
    lag = tail - 1
    span = -(-(samples + MOVE - 1) // LANES) * LANES
    rows = samples // LANES
    pitch = aligned.shape[0] // (stations * count)
    block_rows = block_len // LANES

    for s in range(stations):
        for c in range(comps):
            line = wave_ref[s, c : c + 1, :]
            base = jnp.broadcast_to(line, (16, width))
            for g in range(LANES // 16):
                amount = (16 * g - lag) % width
                hankel[(s * comps + c) * LANES + 16 * g : (s * comps + c) * LANES + 16 * g + 16, :] = pltpu.roll(
                    base, amount, 1, stride=1, stride_axis=0
                )

    for s in range(stations):
        wide = wave_ref[s].astype(jnp.float32)
        square = jnp.sum(wide * wide, axis=0, keepdims=True)
        windows = {1: square}
        step = 1
        while 2 * step <= taps:
            windows[2 * step] = windows[step] + pltpu.roll(windows[step], width - step, 1)
            step *= 2
        energy, start = None, 0
        for size in sorted(windows, reverse=True):
            if start + size <= taps:
                piece = windows[size]
                piece = piece if start == 0 else pltpu.roll(piece, width - start, 1)
                energy = piece if energy is None else energy + piece
                start += size
        inverse = jnp.where(energy > 0.0, lax.rsqrt(energy + eps_energy), 0.0)
        bank = bank_ref[s]
        wide_bank = bank.astype(jnp.float32)
        scale = lax.rsqrt(jnp.sum(wide_bank * wide_bank, axis=1, keepdims=True) + eps_energy)
        for first in range(0, span, 256):
            size = min(256, span - first)
            pieces = []
            for c in range(comps):
                top = (s * comps + c) * LANES
                for q in range(whole):
                    left = first + (whole - q) * LANES
                    pieces.append(hankel[top : top + LANES, left : left + size])
                pieces.append(hankel[top : top + tail, first : first + size])
            product = jnp.dot(bank, jnp.concatenate(pieces, axis=0), preferred_element_type=jnp.float32)
            product = product * scale * inverse[:, first : first + size]
            for x in range(size // LANES):
                for g in range(0, count, 8):
                    aligned[pl.ds((s * count + g) * pitch + first // LANES + x, 8, stride=pitch), :] = product[
                        g : g + 8, x * LANES : (x + 1) * LANES
                    ]

    lane = lax.broadcasted_iota(jnp.int32, (block_rows, LANES), 1)
    for t in range(count):
        for b in range(rows // block_rows):
            total = None
            for s in range(stations):
                move = moves[s, t]
                high = lax.shift_right_logical(move, 7)
                low = lax.bitwise_and(move, LANES - 1)
                at = (s * count + t) * pitch + b * block_rows + high
                here = aligned[pl.ds(at, block_rows), :]
                after = aligned[pl.ds(at + 1, block_rows), :]
                merged = jnp.where(lane >= low, here, after)
                turned = pltpu.roll(merged, lax.rem(LANES - low, LANES), 1)
                term = flags[s, b].astype(jnp.float32) * turned
                total = term if total is None else total + term
            sums[t * rows + b * block_rows : t * rows + (b + 1) * block_rows, :] = total

    for x in range(rows):
        for g in range(0, count, 8):
            out_ref[g : g + 8, x * LANES : (x + 1) * LANES] = sums[pl.ds(g * rows + x, 8, stride=rows), :]


def shards(data, templates, moveouts, mask):
    stations, comps, samples = data.shape
    count, length = templates.shape[1], templates.shape[3]
    trailing = length + MOVE - 1
    blocks = mask.shape[1]
    block_len = samples // blocks
    following = shifted(data[:, :, :trailing], "tm", -1)
    width = -(-(samples + trailing) // LANES) * LANES + LANES
    wave = jnp.concatenate(
        [data, following, jnp.zeros((stations, comps, width - samples - trailing), data.dtype)], axis=2
    )
    bank = templates[..., ::-1].reshape(stations, count, comps * length)
    rows = samples // LANES
    pitch = -(-(rows + MOVE // LANES + 2) // 8) * 8
    sizes = (stations, comps, length, count, samples, block_len)
    partial = pl.pallas_call(
        functools.partial(correlate, sizes=sizes),
        out_shape=jax.ShapeDtypeStruct((count, samples), jnp.float32),
        in_specs=[
            pl.BlockSpec(memory_space=pltpu.SMEM),
            pl.BlockSpec(memory_space=pltpu.SMEM),
            pl.BlockSpec(memory_space=pltpu.VMEM),
            pl.BlockSpec(memory_space=pltpu.VMEM),
        ],
        out_specs=pl.BlockSpec(memory_space=pltpu.VMEM),
        scratch_shapes=[
            pltpu.VMEM((stations * comps * LANES, width), jnp.bfloat16),
            pltpu.VMEM((stations * count * pitch, LANES), jnp.float32),
            pltpu.VMEM((count * rows, LANES), jnp.float32),
        ],
        compiler_params=pltpu.CompilerParams(vmem_limit_bytes=40 * 2**20),
        name="correlate",
    )(moveouts, mask, wave, bank)

    live = jnp.sum(mask.astype(jnp.float32), axis=0)
    number = lax.axis_size("sta")
    if number > 4:
        summed, counts = lax.psum((partial, live), "sta")
    else:
        coded = (partial * WIRE_SCALE).astype(jnp.float16)
        summed, counts = partial, live
        for step in range(1, number):
            pairs = [(k, k ^ step) for k in range(number)]
            counts = counts + lax.ppermute(live, "sta", pairs)
        for step in range(number - 1, 0, -1):
            pairs = [(k, k ^ step) for k in range(number)]
            summed = summed + lax.ppermute(coded, "sta", pairs).astype(jnp.float32) * (1.0 / WIRE_SCALE)
    factor = math.sqrt(comps * length) * lax.rsqrt(counts)
    return summed * jnp.repeat(factor, block_len)[None, :]


def solution(mesh):
    placed = (
        P(("grp", "sta"), None, "tm"),
        P(("grp", "sta"), "comp", None, None),
        P(("grp", "sta"), "comp"),
        P(("grp", "sta"), "tm"),
    )
    return jax.shard_map(
        shards, mesh=mesh, in_specs=placed, out_specs=P(("grp", "comp"), "tm"), check_vma=False
    )
```

time: 1220 us -> 30 us (0.02)
  local copies, waits for them, and re-layouts: 1120 us -> 3.27 us
  waiting for transfers between devices: 34.7 us -> 9.89 us
  loops' own time: 14.1 us -> 0 us
  blocking collectives: 14 us -> 0 us
  between operations: 13.5 us -> 0.15 us
  matrix products: 12.9 us -> 0 us
    gather x4 -> x0, local copies, waits for them, and re-layouts: 1040 us -> none  [one_station(): jnp.take_along_axis(normalized, shifts[:, None] + offsets[None, :], axis=1)]
    another operation x900 -> x0, local copies, waits for them, and re-layouts: 81.7 us -> none  [add_taps(): jnp.stack([lax.dynamic_slice_in_dim(waveform, first_tap + offset, span, 1...]
    psum x1 -> x0, waiting for transfers between devices: 34.7 us -> none  [shards(): summed, total_counts = lax.psum((running, live_counts), 'sta')]
    another operation x3 -> x0, loops' own time: 14.1 us -> none  [the longest x2 13.8 us: one_station(): products, energy = lax.fori_loop(0, groups, add_taps, start)]
    psum x1 -> x0, blocking collectives: 14 us -> none  [shards(): summed, total_counts = lax.psum((running, live_counts), 'sta')]
    dot_general x50 -> x0, matrix products: 12.9 us -> none  [add_taps(): jnp.einsum('tcu,cup->tp', taps, pieces, preferred_element_type=jnp.float32)]
  transfers between devices with their start and end apart: 2 -> 7, of which waited for: 1 -> 3; matrix products, arithmetic and copies ran while one was open for 0% -> 11% of each run, Pallas kernels for 0% -> 0%
where the time goes in v1:
time: 30 us; the launch traced here: 29.7 us
  starting transfers between devices  11.5 us (38%)
  waiting for transfers between devices  9.89 us (33%)
  Pallas kernels  3.32 us (11%)
  local copies, waits for them, and re-layouts  3.27 us (11%)
  other arithmetic  1.57 us (5%)
    ppermute x3, waiting for transfers between devices, shards(): lax.ppermute(coded, 'sta', pairs).astype(jnp.float32) * (1.0 / WIRE_SCALE)  8.09 us
    ppermute x3, starting transfers between devices, shards(): counts = counts + lax.ppermute(live, 'sta', pairs)  5.74 us
    ppermute x3, starting transfers between devices, shards(): lax.ppermute(coded, 'sta', pairs).astype(jnp.float32) * (1.0 / WIRE_SCALE)  4.45 us
    pallas_call x1, Pallas kernels, shards(): pl.pallas_call(functools.partial(correlate, sizes=sizes), out_shape=jax.S...  3.32 us
    unnamed x9, local copies, waits for them, and re-layouts  2.87 us
    ppermute x1, waiting for transfers between devices, shifted(): lax.ppermute(value, axis, [(source, source + steps) for source in range(f...  1.79 us
    ppermute x1, starting transfers between devices, shifted(): lax.ppermute(value, axis, [(source, source + steps) for source in range(f...  1.29 us
    mul x1, other arithmetic, shards(): return summed * jnp.repeat(factor, block_len)[None, :]  0.8 us
  transfers between devices with their start and end apart: 7, of which 3 were waited for; matrix products, arithmetic and copies ran while one was open for 11% of the time, Pallas kernels for 0%

profile of v1, /device:TPU:0, one launch (start us, length us, event | category | flops | bytes accessed | tf_op | source)
XLA Modules:
  0.0 29.7 jit_solution(1176826921526518284)
XLA Ops:
  0.0 0.7 %convert_reduce_fusion = f32[2]{0:T(128)S(1)} fusion(s32[2,2]{1,0:T(2,128)} %flags.1), kind=kLoop, calls=%fused_computation.5 | loop fusion | flops 6 | bytes 24 | tf_op jit(solution)/shard_map/reduce_sum | solution.py:137
  0.7 5.1 %collective-permute-start.6 = (f32[2]{0:T(128)S(1)}, f32[2]{0:T(128)S(1)}, u32[]{:S(2)}, u32[]{:S(2)}) collective-permute-start(f32[2]{0:T(128)S(1)} %convert_reduce_fusion), channel_id=1, source_target_pairs={{0,12},{4,8},{8,4},{12,0},{1,13},{5,9},{9,5},{13,1},{2,14},{6,10},... | collective-permute-start | bytes 32 | tf_op jit(solution)/shard_map/ppermute | solution.py:146
  5.8 0.0 collective-permute-start.5
  5.8 0.6 %collective-permute-start.4 = (f32[2]{0:T(128)S(1)}, f32[2]{0:T(128)S(1)}, u32[]{:S(2)}, u32[]{:S(2)}) collective-permute-start(f32[2]{0:T(128)S(1)} %convert_reduce_fusion), channel_id=1, source_target_pairs={{0,4},{4,0},{8,12},{12,8},{1,5},{5,1},{9,13},{13,9},{2,6},{6,2},{1... | collective-permute-start | bytes 32 | tf_op jit(solution)/shard_map/ppermute | solution.py:146
  6.4 0.8 %copy.9 = bf16[2,3,2048]{2,1,0:T(4,128)(2,1)S(1)} copy(bf16[2,3,2048]{2,0,1:T(2,128)(2,1)} %param.4) | data formatting | bytes 49152 | tf_op args[0]
  7.2 1.3 %collective-permute-start = (bf16[2,3,1024]{2,1,0:T(4,128)(2,1)S(1)}, bf16[2,3,1024]{2,1,0:T(4,128)(2,1)S(1)}, u32[]{:S(2)}, u32[]{:S(2)}) collective-permute-start(bf16[2,3,1024]{2,1,0:T(4,128)(2,1)S(1)} %slice.4), channel_id=1, source_target_pairs={{2,0},{3,1},{6,4},{7,5},{10,8},{11,9},{14,12},{15,13},{18,16},{19,... | collective-permute-start | bytes 36872 | tf_op jit(solution)/shard_map/ppermute | solution.py:21
  8.5 1.9 %reverse = bf16[2,32,3,512]{3,1,2,0:T(8,128)(2,1)S(1)} reverse(bf16[2,32,3,512]{3,1,2,0:T(8,128)(2,1)} %bitcast.6), dimensions={3} | reverse | bytes 393216
  10.4 0.1 slice.5
  10.6 0.2 copy.10
  10.7 0.2 reshape.4.bank_ref
  11.0 0.0 collective-permute-done.6
  11.0 0.0 collective-permute-done.5
  11.0 0.0 collective-permute-done.4
  11.0 0.0 copy-start
  11.0 0.0 copy-start.1
  11.1 1.8 %collective-permute-done = bf16[2,3,1024]{2,1,0:T(4,128)(2,1)S(1)} collective-permute-done((bf16[2,3,1024]{2,1,0:T(4,128)(2,1)S(1)}, bf16[2,3,1024]{2,1,0:T(4,128)(2,1)S(1)}, u32[]{:S(2)}, u32[]{:S(2)}) %collective-permute-start) | collective-permute-done | bytes 12320 | tf_op jit(solution)/shard_map/ppermute | solution.py:21
  12.9 0.0 copy-done
  12.9 0.0 copy-done.1
  12.9 3.3 %correlate.1 = f32[32,2048]{1,0:T(8,128)S(1)} custom-call(s32[2,32]{1,0:T(2,128)S(1)} %copy-done, s32[2,2]{1,0:T(2,128)S(1)} %copy-done.1, bf16[2,3,3200]{2,1,0:T(4,128)(2,1)S(1)} %maximum_maximum_fusion.wave_ref, bf16[2,32,1200]{2,1,0:T(8,128)(2,1)S(1)} %reshape.4.bank_ref), custom_call_target="tpu_custom_call" | custom-call | tf_op jit(solution)/shard_map/correlate/pallas_call | solution.py:118
  16.3 1.4 %collective-permute-start.3 = (f16[32,2048]{1,0:T(8,128)(2,1)S(1)}, f16[32,2048]{1,0:T(8,128)(2,1)S(1)}, u32[]{:S(2)}, u32[]{:S(2)}) collective-permute-start(f16[32,2048]{1,0:T(8,128)(2,1)S(1)} %multiply_convert_fusion), channel_id=1, source_target_pairs={{0,4},{4,0},{8,12},{12,8},{1,5},{5,1},{9,13},{13,9},{2,6},{6,2},{1... | collective-permute-start | bytes 393224 | tf_op jit(solution)/shard_map/ppermute | solution.py:149
  17.7 2.9 %collective-permute-start.2 = (f16[32,2048]{1,0:T(8,128)(2,1)S(1)}, f16[32,2048]{1,0:T(8,128)(2,1)S(1)}, u32[]{:S(2)}, u32[]{:S(2)}) collective-permute-start(f16[32,2048]{1,0:T(8,128)(2,1)S(1)} %multiply_convert_fusion), channel_id=1, source_target_pairs={{0,8},{4,12},{8,0},{12,4},{1,9},{5,13},{9,1},{13,5},{2,10},{6,14},... | collective-permute-start | bytes 393224 | tf_op jit(solution)/shard_map/ppermute | solution.py:149
  20.6 0.1 collective-permute-start.1
  20.7 0.1 broadcast_bitcast_fusion
  20.8 0.9 %collective-permute-done.3 = f16[32,2048]{1,0:T(8,128)(2,1)S(1)} collective-permute-done((f16[32,2048]{1,0:T(8,128)(2,1)S(1)}, f16[32,2048]{1,0:T(8,128)(2,1)S(1)}, u32[]{:S(2)}, u32[]{:S(2)}) %collective-permute-start.3) | collective-permute-done | bytes 131104 | tf_op jit(solution)/shard_map/ppermute | solution.py:149
  21.7 7.2 %collective-permute-done.2 = f16[32,2048]{1,0:T(8,128)(2,1)S(1)} collective-permute-done((f16[32,2048]{1,0:T(8,128)(2,1)S(1)}, f16[32,2048]{1,0:T(8,128)(2,1)S(1)}, u32[]{:S(2)}, u32[]{:S(2)}) %collective-permute-start.2) | collective-permute-done | bytes 131104 | tf_op jit(solution)/shard_map/ppermute | solution.py:149
  28.9 0.0 collective-permute-done.1
  28.9 0.8 %add_multiply_fusion = f32[32,2048]{1,0:T(8,128)} fusion(f16[32,2048]{1,0:T(8,128)(2,1)S(1)} %collective-permute-done.3, f16[32,2048]{1,0:T(8,128)(2,1)S(1)} %collective-permute-done.2, f32[32,2048]{1,0:T(8,128)S(1)} %correlate.1, f16[32,2048]{1,0:T(8,128)(2,1)S(1)} %collective-permute-done.1, f32[2048]{0:T(1024)S(1)} %bitcast.7), kind=kLoop, calls=%fused_computation | loop fusion | flops 655360 | bytes 925696 | tf_op jit(solution)/shard_map/mul | solution.py:151
  (7 shorter events, 0.1 us)
Async XLA Ops:
  0.7 10.3 %collective-permute-start.6 = (f32[2]{0:T(128)S(1)}, f32[2]{0:T(128)S(1)}, u32[]{:S(2)}, u32[]{:S(2)}) collective-permute-start(f32[2]{0:T(128)S(1)} %convert_reduce_fusion), channel_id=1, source_target_pairs={{0,12},{4,8},{8,4},{12,0},{1,13},{5,9},{9,5},{13,1},{2,14},{6,10},... | collective-permute-start | bytes 32 | tf_op jit(solution)/shard_map/ppermute | solution.py:146
  5.8 5.2 %collective-permute-start.5 = (f32[2]{0:T(128)S(1)}, f32[2]{0:T(128)S(1)}, u32[]{:S(2)}, u32[]{:S(2)}) collective-permute-start(f32[2]{0:T(128)S(1)} %convert_reduce_fusion), channel_id=1, source_target_pairs={{0,8},{4,12},{8,0},{12,4},{1,9},{5,13},{9,1},{13,5},{2,10},{6,14},... | collective-permute-start | bytes 32 | tf_op jit(solution)/shard_map/ppermute | solution.py:146
  5.8 5.2 %collective-permute-start.4 = (f32[2]{0:T(128)S(1)}, f32[2]{0:T(128)S(1)}, u32[]{:S(2)}, u32[]{:S(2)}) collective-permute-start(f32[2]{0:T(128)S(1)} %convert_reduce_fusion), channel_id=1, source_target_pairs={{0,4},{4,0},{8,12},{12,8},{1,5},{5,1},{9,13},{13,9},{2,6},{6,2},{1... | collective-permute-start | bytes 32 | tf_op jit(solution)/shard_map/ppermute | solution.py:146
  7.2 5.6 %collective-permute-start = (bf16[2,3,1024]{2,1,0:T(4,128)(2,1)S(1)}, bf16[2,3,1024]{2,1,0:T(4,128)(2,1)S(1)}, u32[]{:S(2)}, u32[]{:S(2)}) collective-permute-start(bf16[2,3,1024]{2,1,0:T(4,128)(2,1)S(1)} %slice.4), channel_id=1, source_target_pairs={{2,0},{3,1},{6,4},{7,5},{10,8},{11,9},{14,12},{15,13},{18,16},{19,... | collective-permute-start | bytes 36872 | tf_op jit(solution)/shard_map/ppermute | solution.py:21
  11.0 1.9 %copy-start = (s32[2,32]{1,0:T(2,128)S(1)}, s32[2,32]{1,0:T(2,128)}, u32[]{:S(2)}) copy-start(s32[2,32]{1,0:T(2,128)} %moves.1) | copy-start | bytes 772
  11.0 1.9 %copy-start.1 = (s32[2,2]{1,0:T(2,128)S(1)}, s32[2,2]{1,0:T(2,128)}, u32[]{:S(2)}) copy-start(s32[2,2]{1,0:T(2,128)} %flags.1) | copy-start | bytes 52
  16.3 5.4 %collective-permute-start.3 = (f16[32,2048]{1,0:T(8,128)(2,1)S(1)}, f16[32,2048]{1,0:T(8,128)(2,1)S(1)}, u32[]{:S(2)}, u32[]{:S(2)}) collective-permute-start(f16[32,2048]{1,0:T(8,128)(2,1)S(1)} %multiply_convert_fusion), channel_id=1, source_target_pairs={{0,4},{4,0},{8,12},{12,8},{1,5},{5,1},{9,13},{13,9},{2,6},{6,2},{1... | collective-permute-start | bytes 393224 | tf_op jit(solution)/shard_map/ppermute | solution.py:149
  17.7 11.2 %collective-permute-start.2 = (f16[32,2048]{1,0:T(8,128)(2,1)S(1)}, f16[32,2048]{1,0:T(8,128)(2,1)S(1)}, u32[]{:S(2)}, u32[]{:S(2)}) collective-permute-start(f16[32,2048]{1,0:T(8,128)(2,1)S(1)} %multiply_convert_fusion), channel_id=1, source_target_pairs={{0,8},{4,12},{8,0},{12,4},{1,9},{5,13},{9,1},{13,5},{2,10},{6,14},... | collective-permute-start | bytes 393224 | tf_op jit(solution)/shard_map/ppermute | solution.py:149
  20.6 8.2 %collective-permute-start.1 = (f16[32,2048]{1,0:T(8,128)(2,1)S(1)}, f16[32,2048]{1,0:T(8,128)(2,1)S(1)}, u32[]{:S(2)}, u32[]{:S(2)}) collective-permute-start(f16[32,2048]{1,0:T(8,128)(2,1)S(1)} %multiply_convert_fusion), channel_id=1, source_target_pairs={{0,12},{4,8},{8,4},{12,0},{1,13},{5,9},{9,5},{13,1},{2,14},{6,10},... | collective-permute-start | bytes 393224 | tf_op jit(solution)/shard_map/ppermute | solution.py:149

commit v2 on v0

v2 whole, which is shorter than its diff:
```python
import functools
import math

import jax
import jax.numpy as jnp
from jax import lax
from jax.experimental import pallas as pl
from jax.experimental.pallas import tpu as pltpu
from jax.sharding import PartitionSpec as P

MOVE = 625

eps_energy = 1e-06
LANES = 128
GROUP = 16
WIRE_SCALE = 2.0**13


def from_next(value, axis):
    count = lax.axis_size(axis)
    arrived = lax.ppermute(value, axis, [(k, (k - 1) % count) for k in range(count)])
    return jnp.where(lax.axis_index(axis) == count - 1, jnp.zeros_like(arrived), arrived)


def turn_groups(rows):
    width = rows.shape[1]
    source = lax.broadcasted_iota(jnp.int32, (width, width), 0)
    target = lax.broadcasted_iota(jnp.int32, (width, width), 1)
    swap = jnp.where(source == (target // GROUP) * GROUP + (GROUP - 1 - target % GROUP), 1.0, 0.0)
    return jnp.dot(rows, swap.astype(rows.dtype), preferred_element_type=jnp.float32).astype(rows.dtype)


def prepare(bank_ref, turned_ref, scale_ref):
    stations, comps, count, taps = bank_ref.shape
    whole = taps // LANES
    tail = taps - whole * LANES
    chunks = []
    for s in range(stations):
        energy = None
        for c in range(comps):
            wide = bank_ref[s, c].astype(jnp.float32)
            term = jnp.sum(wide * wide, axis=1, keepdims=True)
            energy = term if energy is None else energy + term
            for q in range(whole):
                chunks.append(bank_ref[s, c, :, q * LANES : (q + 1) * LANES])
        scale_ref[s] = jnp.broadcast_to(lax.rsqrt(energy + eps_energy), (count, LANES))
    turned = turn_groups(jnp.concatenate(chunks, axis=0))
    for s in range(stations):
        for n in range(comps * whole):
            first = (s * comps * whole + n) * count
            turned_ref[s, :, n * LANES : (n + 1) * LANES] = turned[first : first + count]
        for c in range(comps):
            left = comps * whole * LANES + c * tail
            turned_ref[s, :, left : left + tail] = turn_groups(bank_ref[s, c, :, whole * LANES :])


def fill_hankel(window, hankel, stations, comps):
    for s in range(stations):
        for c in range(comps):
            line = window(s, c)
            width = line.shape[1]
            base = jnp.broadcast_to(line, (GROUP, width))
            for g in range(LANES // GROUP):
                amount = (width - GROUP * g - (GROUP - 1)) % width
                top = (s * comps + c) * LANES + GROUP * g
                hankel[top : top + GROUP, :] = pltpu.roll(base, amount, 1, stride=1, stride_axis=0)


def window_energy(square, taps):
    width = square.shape[1]
    sums, size = {1: square}, 1
    while 2 * size <= taps:
        sums[2 * size] = sums[size] + pltpu.roll(sums[size], width - size, 1)
        size *= 2
    energy, start = None, 0
    for size in sorted(sums, reverse=True):
        if start + size <= taps:
            piece = sums[size] if start == 0 else pltpu.roll(sums[size], width - start, 1)
            energy = piece if energy is None else energy + piece
            start += size
    return energy


def inverse_energy(square, taps):
    energy = window_energy(square, taps)
    return jnp.where(energy > 0.0, lax.rsqrt(energy + eps_energy), 0.0)


def products(inverse, turned_ref, scale_ref, hankel, taps, comps, tiles, put):
    stations, count, depth = turned_ref.shape
    whole = taps // LANES
    tail = taps - whole * LANES
    span = tiles * LANES
    for s in range(stations):
        pieces = []
        for c in range(comps):
            top = (s * comps + c) * LANES
            for q in range(whole):
                pieces.append(hankel[top : top + LANES, q * LANES : q * LANES + span])
        for c in range(comps):
            top = (s * comps + c) * LANES
            pieces.append(hankel[top : top + tail, whole * LANES : whole * LANES + span])
        product = jnp.dot(turned_ref[s], jnp.concatenate(pieces, axis=0), preferred_element_type=jnp.float32)
        product = product * inverse[s : s + 1, :span]
        for x in range(tiles):
            for g in range(0, count, 8):
                tile = product[g : g + 8, x * LANES : (x + 1) * LANES] * scale_ref[s, g : g + 8, :]
                put(s * count + g, x, tile)


def align(moves, flags, block, aligned, sums, out_ref, rows):
    stations, count = moves.shape
    pitch = aligned.shape[0] // (stations * count)
    lane = lax.broadcasted_iota(jnp.int32, (rows, LANES), 1)
    for t in range(count):
        total = None
        for s in range(stations):
            move = moves[s, t]
            high = lax.shift_right_logical(move, 7)
            low = lax.bitwise_and(move, LANES - 1)
            at = (s * count + t) * pitch + high
            merged = jnp.where(lane >= low, aligned[pl.ds(at, rows), :], aligned[pl.ds(at + 1, rows), :])
            term = flags[s, block].astype(jnp.float32) * pltpu.roll(merged, LANES - low, 1)
            total = term if total is None else total + term
        sums[t * rows : (t + 1) * rows, :] = total
    for x in range(rows):
        for g in range(0, count, 8):
            out_ref[g : g + 8, x * LANES : (x + 1) * LANES] = sums[pl.ds(g * rows + x, 8, stride=rows), :]


def put_counts(flags, out_ref, left):
    lane = lax.broadcasted_iota(jnp.int32, (out_ref.shape[0], LANES), 1)
    counts = jnp.zeros(lane.shape, jnp.float32)
    for b in range(flags.shape[1]):
        live = sum(flags[s, b] for s in range(flags.shape[0])).astype(jnp.float32)
        counts = jnp.where(lane == b, live, counts)
    out_ref[:, left : left + LANES] = counts


def first_block(
    moves, flags, wave_hbm, bank_hbm, out_ref, later_ref, turned_ref, scale_ref, kept_ref,
    wave_ref, bank_ref, hankel, aligned, sums, ready,
):
    comps, stations, samples = wave_ref.shape
    count, taps = bank_ref.shape[2:]
    rows = sums.shape[0] // count
    length = rows * LANES
    pitch = aligned.shape[0] // (stations * count)
    kept = kept_ref.shape[0] // (stations * count)
    wave_copy = pltpu.make_async_copy(wave_hbm, wave_ref, ready.at[0])
    bank_copy = pltpu.make_async_copy(bank_hbm, bank_ref, ready.at[1])
    wave_copy.start()
    bank_copy.start()
    put_counts(flags, out_ref, length)
    wave_copy.wait()
    bank_copy.wait()
    later_ref[...] = wave_ref[:, :, samples - later_ref.shape[2] :]

    def window(s, c):
        return wave_ref[c, s : s + 1, : 2 * length]

    fill_hankel(window, hankel, stations, comps)
    wide = wave_ref[:, :, : 2 * length].astype(jnp.float32)
    inverse = inverse_energy(jnp.sum(wide * wide, axis=0), taps)
    prepare(bank_ref, turned_ref, scale_ref)

    def put(first, x, tile):
        aligned[pl.ds(first * pitch + x, 8, stride=pitch), :] = tile
        if rows <= x < rows + kept:
            kept_ref[pl.ds(first * kept + x - rows, 8, stride=kept), :] = tile

    products(inverse, turned_ref, scale_ref, hankel, taps, comps, pitch, put)
    align(moves, flags, 0, aligned, sums, out_ref, rows)


def last_block(
    moves, flags, later_ref, next_ref, turned_ref, scale_ref, kept_ref, out_ref, hankel, aligned, sums, *, taps
):
    comps, stations, own = later_ref.shape
    count, length = out_ref.shape
    rows = length // LANES
    pitch = aligned.shape[0] // (stations * count)
    kept = kept_ref.shape[0] // (stations * count)

    def window(s, c):
        return jnp.concatenate([later_ref[c, s : s + 1, :], next_ref[c, s : s + 1, :length]], axis=1)

    fill_hankel(window, hankel, stations, comps)
    squares = [jnp.sum(part * part, axis=0) for part in (later_ref[...].astype(jnp.float32), next_ref[:, :, :length].astype(jnp.float32))]
    inverse = inverse_energy(jnp.concatenate(squares, axis=1), taps)
    for first in range(0, stations * count, 8):
        for x in range(kept):
            aligned[pl.ds(first * pitch + x, 8, stride=pitch), :] = kept_ref[pl.ds(first * kept + x, 8, stride=kept), :]

    def put(first, x, tile):
        aligned[pl.ds(first * pitch + kept + x, 8, stride=pitch), :] = tile

    products(inverse, turned_ref, scale_ref, hankel, taps, comps, pitch - kept, put)
    align(moves, flags, flags.shape[1] - 1, aligned, sums, out_ref, rows)


def finish(first_ref, last_ref, near_ref, far_ref, out_ref, *, factor):
    length = last_ref.shape[1]
    counts = first_ref[:, length:] + near_ref[:, length : length + LANES]
    lane = lax.broadcasted_iota(jnp.int32, counts.shape, 1)
    sums = first_ref[:, :length] + near_ref[:, :length], last_ref[...] + near_ref[:, length + LANES :] + far_ref[...]
    for b, total in enumerate(sums):
        count = jnp.sum(jnp.where(lane == b, counts, 0.0), axis=1, keepdims=True)
        out_ref[:, b * length : (b + 1) * length] = total * (factor * lax.rsqrt(count))


def shards(data, templates, moveouts, mask):
    stations, comps, samples = data.shape
    count, taps = templates.shape[1], templates.shape[3]
    blocks = mask.shape[1]
    length = samples // blocks
    assert blocks == 2 and length >= taps + MOVE - 1
    wave_own = jnp.transpose(data, (1, 0, 2))
    wave = pltpu.with_memory_space_constraint(wave_own, pltpu.HBM)
    bank = pltpu.with_memory_space_constraint(jnp.transpose(templates, (0, 2, 1, 3)), pltpu.HBM)
    following = from_next(wave_own, "tm")

    rows = length // LANES
    pitch = rows + -(-(MOVE - 1) // LANES)
    kept = (2 * length - taps + 1) // LANES - rows
    smem, vmem = pl.BlockSpec(memory_space=pltpu.SMEM), pl.BlockSpec(memory_space=pltpu.VMEM)
    hbm = pl.BlockSpec(memory_space=pltpu.HBM)
    last_width = 2 * length - kept * LANES

    def scratch(width):
        return [
            pltpu.VMEM((stations * comps * LANES, width), jnp.bfloat16),
            pltpu.VMEM((stations * count * pitch, LANES), jnp.float32),
            pltpu.VMEM((count * rows, LANES), jnp.float32),
        ]

    params = pltpu.CompilerParams(vmem_limit_bytes=32 * 2**20)
    first, later, turned, scale, both = pl.pallas_call(
        first_block,
        out_shape=(
            jax.ShapeDtypeStruct((count, length + LANES), jnp.float32),
            jax.ShapeDtypeStruct((comps, stations, last_width - length), jnp.bfloat16),
            jax.ShapeDtypeStruct((stations, count, comps * taps), jnp.bfloat16),
            jax.ShapeDtypeStruct((stations, count, LANES), jnp.float32),
            jax.ShapeDtypeStruct((stations * count * kept, LANES), jnp.float32),
        ),
        in_specs=[smem, smem, hbm, hbm],
        out_specs=(vmem, vmem, vmem, vmem, vmem),
        scratch_shapes=[pltpu.VMEM(wave.shape, wave.dtype), pltpu.VMEM(bank.shape, bank.dtype)]
        + scratch(2 * length)
        + [pltpu.SemaphoreType.DMA((2,))],
        compiler_params=params,
        name="first_block",
    )(moveouts, mask, wave, bank)
    last = pl.pallas_call(
        functools.partial(last_block, taps=taps),
        out_shape=jax.ShapeDtypeStruct((count, length), jnp.float32),
        in_specs=[smem, smem, vmem, vmem, vmem, vmem, vmem],
        out_specs=vmem,
        scratch_shapes=scratch(last_width),
        compiler_params=params,
        name="last_block",
    )(moveouts, mask, later, following, turned, scale, both)

    number = lax.axis_size("sta")
    if number != 4:
        first, last = lax.psum((first, last), "sta")
        counts = first[:1, length:]
        gain = [math.sqrt(comps * taps) * lax.rsqrt(counts[:, b : b + 1]) for b in range(blocks)]
        return jnp.concatenate([first[:, :length] * gain[0], last * gain[1]], axis=1)

    def exchange(part, step):
        return lax.ppermute(part, "sta", [(k, k ^ step) for k in range(number)])

    def code(part):
        return (part * WIRE_SCALE).astype(jnp.float16)

    def decode(part):
        return part.astype(jnp.float32) * (1.0 / WIRE_SCALE)

    coded_last = code(last)
    far_first = exchange(code(first), 2)
    far = [exchange(coded_last, step) for step in (3, 2)]
    first = first + decode(far_first)
    near = exchange(jnp.concatenate([code(first), coded_last], axis=1), 1)
    return pl.pallas_call(
        functools.partial(finish, factor=math.sqrt(comps * taps)),
        out_shape=jax.ShapeDtypeStruct((count, samples), jnp.float32),
        in_specs=[vmem] * 4,
        out_specs=vmem,
        compiler_params=params,
        name="finish",
    )(first, last, decode(near), decode(far[0]) + decode(far[1]))


def solution(mesh):
    placed = (
        P(("grp", "sta"), None, "tm"),
        P(("grp", "sta"), "comp", None, None),
        P(("grp", "sta"), "comp"),
        P(("grp", "sta"), "tm"),
    )
    return jax.shard_map(
        shards, mesh=mesh, in_specs=placed, out_specs=P(("grp", "comp"), "tm"), check_vma=False
    )
```

time: 1220 us -> 21.6 us (0.02)
  local copies, waits for them, and re-layouts: 1120 us -> 0.01 us
  waiting for transfers between devices: 34.7 us -> 5.3 us
  loops' own time: 14.1 us -> 0 us
  blocking collectives: 14 us -> 0 us
  between operations: 13.5 us -> 0.05 us
  matrix products: 12.9 us -> 0 us
    gather x4 -> x0, local copies, waits for them, and re-layouts: 1040 us -> none  [one_station(): jnp.take_along_axis(normalized, shifts[:, None] + offsets[None, :], axis=1)]
    another operation x900 -> x0, local copies, waits for them, and re-layouts: 81.7 us -> none  [add_taps(): jnp.stack([lax.dynamic_slice_in_dim(waveform, first_tap + offset, span, 1...]
    psum x1 -> x0, waiting for transfers between devices: 34.7 us -> none  [shards(): summed, total_counts = lax.psum((running, live_counts), 'sta')]
    another operation x3 -> x0, loops' own time: 14.1 us -> none  [the longest x2 13.8 us: one_station(): products, energy = lax.fori_loop(0, groups, add_taps, start)]
    psum x1 -> x0, blocking collectives: 14 us -> none  [shards(): summed, total_counts = lax.psum((running, live_counts), 'sta')]
    dot_general x50 -> x0, matrix products: 12.9 us -> none  [add_taps(): jnp.einsum('tcu,cup->tp', taps, pieces, preferred_element_type=jnp.float32)]
  transfers between devices with their start and end apart: 2 -> 5, of which waited for: 1 -> 2; matrix products, arithmetic and copies ran while one was open for 0% -> 1% of each run, Pallas kernels for 0% -> 24%
where the time goes in v2:
time: 21.6 us; the launch traced here: 21.5 us
  starting transfers between devices  10 us (46%)
  Pallas kernels  5.96 us (28%)
  waiting for transfers between devices  5.3 us (25%)
    ppermute x4, starting transfers between devices, exchange(): return lax.ppermute(part, 'sta', [(k, k ^ step) for k in range(number)])  7.07 us
    ppermute x4, waiting for transfers between devices, exchange(): return lax.ppermute(part, 'sta', [(k, k ^ step) for k in range(number)])  5.3 us
    pallas_call x1, Pallas kernels, shards(): pl.pallas_call(first_block, out_shape=(jax.ShapeDtypeStruct((count, lengt...  3.24 us
    ppermute x1, starting transfers between devices, from_next(): lax.ppermute(value, axis, [(k, (k - 1) % count) for k in range(count)])  2.94 us
    pallas_call x1, Pallas kernels, shards(): pl.pallas_call(functools.partial(last_block, taps=taps), out_shape=jax.Sh...  1.91 us
    pallas_call x1, Pallas kernels, shards(): pl.pallas_call(functools.partial(finish, factor=math.sqrt(comps * taps)),...  0.81 us
  transfers between devices with their start and end apart: 5, of which 2 were waited for; matrix products, arithmetic and copies ran while one was open for 1% of the time, Pallas kernels for 24%

profile of v2, /device:TPU:0, one launch (start us, length us, event | category | flops | bytes accessed | tf_op | source)
XLA Modules:
  0.0 21.5 jit_solution(12468414509336886759)
XLA Ops:
  0.0 0.0 copy-start.1
  0.0 0.0 copy-start
  0.0 2.9 %collective-permute-start.1 = (bf16[3,2,2048]{2,1,0:T(2,128)(2,1)}, bf16[3,2,2048]{2,1,0:T(2,128)(2,1)S(1)}, u32[]{:S(2)}, u32[]{:S(2)}) collective-permute-start(bf16[3,2,2048]{2,1,0:T(2,128)(2,1)} %bitcast.3), channel_id=1, source_target_pairs={{0,2},{2,0},{1,3},{3,1},{4,6},{6,4},{5,7},{7,5},{8,10},{10,8},{9,1... | collective-permute-start | bytes 73736 | tf_op jit(solution)/shard_map/ppermute | solution.py:21
  2.9 0.0 copy-done.1
  2.9 0.0 copy-done
  2.9 3.2 %first_block.1 = (f32[32,1152]{1,0:T(8,128)S(1)}, bf16[3,2,512]{2,1,0:T(2,128)(2,1)S(1)}, bf16[2,32,1200]{2,1,0:T(8,128)(2,1)S(1)}, f32[2,32,128]{2,1,0:T(8,128)S(1)}, f32[256,128]{1,0:T(8,128)S(1)}) custom-call(s32[2,32]{1,0:T(2,128)S(1)} %copy-done, s32[2,2]{1,0:T(2,128)S(1)} %copy-done.1, bf16[3,2,2048]{2,1,0:T(2,128)(2,1)} %bitcast.4, ...), custom_call_target="tpu_custom_call" | custom-call | tf_op jit(solution)/shard_map/first_block/pallas_call | solution.py:238
  6.2 2.7 %collective-permute-start = (f16[32,1152]{1,0:T(8,128)(2,1)S(1)}, f16[32,1152]{1,0:T(8,128)(2,1)S(1)}, u32[]{:S(2)}, u32[]{:S(2)}) collective-permute-start(f16[32,1152]{1,0:T(8,128)(2,1)S(1)} %multiply_convert_fusion.1), channel_id=1, source_target_pairs={{0,8},{4,12},{8,0},{12,4},{1,9},{5,13},{9,1},{13,5},{2,10},{6,14},... | collective-permute-start | bytes 221192 | tf_op jit(solution)/shard_map/ppermute | solution.py:273
  8.9 0.0 collective-permute-done.1
  8.9 1.9 %last_block.1.last_ref = f32[32,1024]{1,0:T(8,128)S(1)} custom-call(s32[2,32]{1,0:T(2,128)S(1)} %copy-done, s32[2,2]{1,0:T(2,128)S(1)} %copy-done.1, bf16[3,2,512]{2,1,0:T(2,128)(2,1)S(1)} %get-tuple-element.11.later_ref, bf16[3,2,2048]{2,1,0:T(2,128)(2,1)S(1)} %broadcast_select_fusion.next_ref, bf16[2,32,1200]{2,1,0:T(8,128)(2,1)S(1)} %get-tuple-element.12.turned_ref, ...), custom_call_target="tpu_custom_call" | custom-call | tf_op jit(solution)/shard_map/last_block/pallas_call | solution.py:255
  10.8 0.4 %collective-permute-start.4 = (f16[32,1024]{1,0:T(8,128)(2,1)S(1)}, f16[32,1024]{1,0:T(8,128)(2,1)S(1)}, u32[]{:S(2)}, u32[]{:S(2)}) collective-permute-start(f16[32,1024]{1,0:T(8,128)(2,1)S(1)} %multiply_convert_fusion.2), channel_id=1, source_target_pairs={{0,8},{4,12},{8,0},{12,4},{1,9},{5,13},{9,1},{13,5},{2,10},{6,14},... | collective-permute-start | bytes 196616 | tf_op jit(solution)/shard_map/ppermute | solution.py:273
  11.2 3.6 %collective-permute-start.3 = (f16[32,1024]{1,0:T(8,128)(2,1)S(1)}, f16[32,1024]{1,0:T(8,128)(2,1)S(1)}, u32[]{:S(2)}, u32[]{:S(2)}) collective-permute-start(f16[32,1024]{1,0:T(8,128)(2,1)S(1)} %multiply_convert_fusion.2), channel_id=1, source_target_pairs={{0,12},{4,8},{8,4},{12,0},{1,13},{5,9},{9,5},{13,1},{2,14},{6,10},... | collective-permute-start | bytes 196616 | tf_op jit(solution)/shard_map/ppermute | solution.py:273
  14.8 0.0 collective-permute-done
  14.9 0.4 %collective-permute-start.2 = (f16[32,2176]{1,0:T(8,128)(2,1)S(1)}, f16[32,2176]{1,0:T(8,128)(2,1)S(1)}, u32[]{:S(2)}, u32[]{:S(2)}) collective-permute-start(f16[32,2176]{1,0:T(8,128)(2,1)S(1)} %pad_maximum_fusion), channel_id=1, source_target_pairs={{0,4},{4,0},{8,12},{12,8},{1,5},{5,1},{9,13},{13,9},{2,6},{6,2},{1... | collective-permute-start | bytes 417800 | tf_op jit(solution)/shard_map/ppermute | solution.py:273
  15.3 3.3 %collective-permute-done.4 = f16[32,1024]{1,0:T(8,128)(2,1)S(1)} collective-permute-done((f16[32,1024]{1,0:T(8,128)(2,1)S(1)}, f16[32,1024]{1,0:T(8,128)(2,1)S(1)}, u32[]{:S(2)}, u32[]{:S(2)}) %collective-permute-start.4) | collective-permute-done | bytes 65568 | tf_op jit(solution)/shard_map/ppermute | solution.py:273
  18.6 0.0 collective-permute-done.3
  18.7 2.0 %collective-permute-done.2 = f16[32,2176]{1,0:T(8,128)(2,1)S(1)} collective-permute-done((f16[32,2176]{1,0:T(8,128)(2,1)S(1)}, f16[32,2176]{1,0:T(8,128)(2,1)S(1)}, u32[]{:S(2)}, u32[]{:S(2)}) %collective-permute-start.2) | collective-permute-done | bytes 139296 | tf_op jit(solution)/shard_map/ppermute | solution.py:273
  20.7 0.8 %finish.1 = f32[32,2048]{1,0:T(8,128)} custom-call(f32[32,1152]{1,0:T(8,128)S(1)} %get-tuple-element.16.first_ref, f32[32,1024]{1,0:T(8,128)S(1)} %last_block.1.last_ref, f32[32,2176]{1,0:T(8,128)S(1)} %convert_multiply_fusion.near_ref, f32[32,1024]{1,0:T(8,128)S(1)} %add_multiply_fusion.far_ref), custom_call_target="tpu_custom_call" | custom-call | tf_op jit(solution)/shard_map/finish/pallas_call | solution.py:286
  (7 shorter events, 0.2 us)
Async XLA Ops:
  0.0 2.9 %copy-start.1 = (s32[2,2]{1,0:T(2,128)S(1)}, s32[2,2]{1,0:T(2,128)}, u32[]{:S(2)}) copy-start(s32[2,2]{1,0:T(2,128)} %flags.3) | copy-start | bytes 52
  0.0 2.9 %copy-start = (s32[2,32]{1,0:T(2,128)S(1)}, s32[2,32]{1,0:T(2,128)}, u32[]{:S(2)}) copy-start(s32[2,32]{1,0:T(2,128)} %moves.3) | copy-start | bytes 772
  0.0 8.9 %collective-permute-start.1 = (bf16[3,2,2048]{2,1,0:T(2,128)(2,1)}, bf16[3,2,2048]{2,1,0:T(2,128)(2,1)S(1)}, u32[]{:S(2)}, u32[]{:S(2)}) collective-permute-start(bf16[3,2,2048]{2,1,0:T(2,128)(2,1)} %bitcast.3), channel_id=1, source_target_pairs={{0,2},{2,0},{1,3},{3,1},{4,6},{6,4},{5,7},{7,5},{8,10},{10,8},{9,1... | collective-permute-start | bytes 73736 | tf_op jit(solution)/shard_map/ppermute | solution.py:21
  6.2 8.6 %collective-permute-start = (f16[32,1152]{1,0:T(8,128)(2,1)S(1)}, f16[32,1152]{1,0:T(8,128)(2,1)S(1)}, u32[]{:S(2)}, u32[]{:S(2)}) collective-permute-start(f16[32,1152]{1,0:T(8,128)(2,1)S(1)} %multiply_convert_fusion.1), channel_id=1, source_target_pairs={{0,8},{4,12},{8,0},{12,4},{1,9},{5,13},{9,1},{13,5},{2,10},{6,14},... | collective-permute-start | bytes 221192 | tf_op jit(solution)/shard_map/ppermute | solution.py:273
  10.8 7.8 %collective-permute-start.4 = (f16[32,1024]{1,0:T(8,128)(2,1)S(1)}, f16[32,1024]{1,0:T(8,128)(2,1)S(1)}, u32[]{:S(2)}, u32[]{:S(2)}) collective-permute-start(f16[32,1024]{1,0:T(8,128)(2,1)S(1)} %multiply_convert_fusion.2), channel_id=1, source_target_pairs={{0,8},{4,12},{8,0},{12,4},{1,9},{5,13},{9,1},{13,5},{2,10},{6,14},... | collective-permute-start | bytes 196616 | tf_op jit(solution)/shard_map/ppermute | solution.py:273
  11.2 7.4 %collective-permute-start.3 = (f16[32,1024]{1,0:T(8,128)(2,1)S(1)}, f16[32,1024]{1,0:T(8,128)(2,1)S(1)}, u32[]{:S(2)}, u32[]{:S(2)}) collective-permute-start(f16[32,1024]{1,0:T(8,128)(2,1)S(1)} %multiply_convert_fusion.2), channel_id=1, source_target_pairs={{0,12},{4,8},{8,4},{12,0},{1,13},{5,9},{9,5},{13,1},{2,14},{6,10},... | collective-permute-start | bytes 196616 | tf_op jit(solution)/shard_map/ppermute | solution.py:273
  14.9 5.7 %collective-permute-start.2 = (f16[32,2176]{1,0:T(8,128)(2,1)S(1)}, f16[32,2176]{1,0:T(8,128)(2,1)S(1)}, u32[]{:S(2)}, u32[]{:S(2)}) collective-permute-start(f16[32,2176]{1,0:T(8,128)(2,1)S(1)} %pad_maximum_fusion), channel_id=1, source_target_pairs={{0,4},{4,0},{8,12},{12,8},{1,5},{5,1},{9,13},{13,9},{2,6},{6,2},{1... | collective-permute-start | bytes 417800 | tf_op jit(solution)/shard_map/ppermute | solution.py:273

commit v3 on v2

--- a/solution.py
+++ b/solution.py
@@ -13,6 +13,7 @@
 eps_energy = 1e-06
 LANES = 128
 GROUP = 16
+COUNT_ROWS = 8
 WIRE_SCALE = 2.0**13
 
 
@@ -108,7 +109,7 @@
                 put(s * count + g, x, tile)
 
 
-def align(moves, flags, block, aligned, sums, out_ref, rows):
+def align(moves, flags, block, aligned, out_ref, rows):
     stations, count = moves.shape
     pitch = aligned.shape[0] // (stations * count)
     lane = lax.broadcasted_iota(jnp.int32, (rows, LANES), 1)
@@ -122,38 +123,39 @@
             merged = jnp.where(lane >= low, aligned[pl.ds(at, rows), :], aligned[pl.ds(at + 1, rows), :])
             term = flags[s, block].astype(jnp.float32) * pltpu.roll(merged, LANES - low, 1)
             total = term if total is None else total + term
-        sums[t * rows : (t + 1) * rows, :] = total
-    for x in range(rows):
-        for g in range(0, count, 8):
-            out_ref[g : g + 8, x * LANES : (x + 1) * LANES] = sums[pl.ds(g * rows + x, 8, stride=rows), :]
-
-
-def put_counts(flags, out_ref, left):
-    lane = lax.broadcasted_iota(jnp.int32, (out_ref.shape[0], LANES), 1)
+        out_ref[t * rows : (t + 1) * rows, :] = total
+
+
+def put_counts(flags, out_ref, top):
+    lane = lax.broadcasted_iota(jnp.int32, (COUNT_ROWS, LANES), 1)
     counts = jnp.zeros(lane.shape, jnp.float32)
     for b in range(flags.shape[1]):
         live = sum(flags[s, b] for s in range(flags.shape[0])).astype(jnp.float32)
         counts = jnp.where(lane == b, live, counts)
-    out_ref[:, left : left + LANES] = counts
+    out_ref[top : top + COUNT_ROWS, :] = counts
+
+
+def fetch(pairs, ready):
+    copies = [pltpu.make_async_copy(source, target, ready.at[n]) for n, (source, target) in enumerate(pairs)]
+    for copy in copies:
+        copy.start()
+    return copies
 
 
 def first_block(
-    moves, flags, wave_hbm, bank_hbm, out_ref, later_ref, turned_ref, scale_ref, kept_ref,
-    wave_ref, bank_ref, hankel, aligned, sums, ready,
+    moves_hbm, flags_hbm, wave_hbm, bank_hbm, out_ref, later_ref, turned_ref, scale_ref, kept_ref,
+    wave_ref, bank_ref, moves, flags, hankel, aligned, ready,
 ):
     comps, stations, samples = wave_ref.shape
     count, taps = bank_ref.shape[2:]
-    rows = sums.shape[0] // count
+    rows = (out_ref.shape[0] - COUNT_ROWS) // count
     length = rows * LANES
     pitch = aligned.shape[0] // (stations * count)
     kept = kept_ref.shape[0] // (stations * count)
-    wave_copy = pltpu.make_async_copy(wave_hbm, wave_ref, ready.at[0])
-    bank_copy = pltpu.make_async_copy(bank_hbm, bank_ref, ready.at[1])
-    wave_copy.start()
-    bank_copy.start()
-    put_counts(flags, out_ref, length)
-    wave_copy.wait()
-    bank_copy.wait()
+    copies = fetch(((wave_hbm, wave_ref), (bank_hbm, bank_ref), (moves_hbm, moves), (flags_hbm, flags)), ready)
+    for copy in copies:
+        copy.wait()
+    put_counts(flags, out_ref, count * rows)
     later_ref[...] = wave_ref[:, :, samples - later_ref.shape[2] :]
 
     def window(s, c):
@@ -170,17 +172,20 @@
             kept_ref[pl.ds(first * kept + x - rows, 8, stride=kept), :] = tile
 
     products(inverse, turned_ref, scale_ref, hankel, taps, comps, pitch, put)
-    align(moves, flags, 0, aligned, sums, out_ref, rows)
+    align(moves, flags, 0, aligned, out_ref, rows)
 
 
 def last_block(
-    moves, flags, later_ref, next_ref, turned_ref, scale_ref, kept_ref, out_ref, hankel, aligned, sums, *, taps
+    moves_hbm, flags_hbm, later_ref, next_ref, turned_ref, scale_ref, kept_ref, out_ref,
+    moves, flags, hankel, aligned, ready, *, taps,
 ):
     comps, stations, own = later_ref.shape
-    count, length = out_ref.shape
-    rows = length // LANES
+    count = scale_ref.shape[1]
+    rows = out_ref.shape[0] // count
+    length = rows * LANES
     pitch = aligned.shape[0] // (stations * count)
     kept = kept_ref.shape[0] // (stations * count)
+    copies = fetch(((moves_hbm, moves), (flags_hbm, flags)), ready)
 
     def window(s, c):
         return jnp.concatenate([later_ref[c, s : s + 1, :], next_ref[c, s : s + 1, :length]], axis=1)
@@ -196,17 +201,27 @@
         aligned[pl.ds(first * pitch + kept + x, 8, stride=pitch), :] = tile
 
     products(inverse, turned_ref, scale_ref, hankel, taps, comps, pitch - kept, put)
-    align(moves, flags, flags.shape[1] - 1, aligned, sums, out_ref, rows)
-
-
-def finish(first_ref, last_ref, near_ref, far_ref, out_ref, *, factor):
-    length = last_ref.shape[1]
-    counts = first_ref[:, length:] + near_ref[:, length : length + LANES]
+    for copy in copies:
+        copy.wait()
+    align(moves, flags, flags.shape[1] - 1, aligned, out_ref, rows)
+
+
+def finish(first_ref, near_ref, last_ref, far_ref, out_ref, sums, *, factor):
+    count, samples = out_ref.shape
+    size = last_ref.shape[0]
+    rows = size // count
+    counts = first_ref[size:, :] + near_ref[size:, :]
     lane = lax.broadcasted_iota(jnp.int32, counts.shape, 1)
-    sums = first_ref[:, :length] + near_ref[:, :length], last_ref[...] + near_ref[:, length + LANES :] + far_ref[...]
-    for b, total in enumerate(sums):
-        count = jnp.sum(jnp.where(lane == b, counts, 0.0), axis=1, keepdims=True)
-        out_ref[:, b * length : (b + 1) * length] = total * (factor * lax.rsqrt(count))
+    for b, (own_ref, other_ref) in enumerate(((first_ref, near_ref), (last_ref, far_ref))):
+        live = jnp.sum(jnp.where(lane == b, counts, 0.0), axis=1, keepdims=True)
+        gain = jnp.broadcast_to(factor * lax.rsqrt(live), (COUNT_ROWS, LANES))
+        for top in range(0, size, COUNT_ROWS):
+            part = slice(top, top + COUNT_ROWS)
+            sums[part, :] = (own_ref[part, :] + other_ref[part, :]) * gain
+        for x in range(rows):
+            left = (b * rows + x) * LANES
+            for g in range(0, count, 8):
+                out_ref[g : g + 8, left : left + LANES] = sums[pl.ds(g * rows + x, 8, stride=rows), :]
 
 
 def shards(data, templates, moveouts, mask):
@@ -223,51 +238,47 @@
     rows = length // LANES
     pitch = rows + -(-(MOVE - 1) // LANES)
     kept = (2 * length - taps + 1) // LANES - rows
-    smem, vmem = pl.BlockSpec(memory_space=pltpu.SMEM), pl.BlockSpec(memory_space=pltpu.VMEM)
-    hbm = pl.BlockSpec(memory_space=pltpu.HBM)
+    vmem = pl.BlockSpec(memory_space=pltpu.VMEM)
+    hbm = pl.BlockSpec(memory_space=pl.ANY)
     last_width = 2 * length - kept * LANES
 
     def scratch(width):
         return [
+            pltpu.SMEM(moveouts.shape, moveouts.dtype),
+            pltpu.SMEM(mask.shape, mask.dtype),
             pltpu.VMEM((stations * comps * LANES, width), jnp.bfloat16),
             pltpu.VMEM((stations * count * pitch, LANES), jnp.float32),
-            pltpu.VMEM((count * rows, LANES), jnp.float32),
         ]
 
     params = pltpu.CompilerParams(vmem_limit_bytes=32 * 2**20)
     first, later, turned, scale, both = pl.pallas_call(
         first_block,
         out_shape=(
-            jax.ShapeDtypeStruct((count, length + LANES), jnp.float32),
+            jax.ShapeDtypeStruct((count * rows + COUNT_ROWS, LANES), jnp.float32),
             jax.ShapeDtypeStruct((comps, stations, last_width - length), jnp.bfloat16),
             jax.ShapeDtypeStruct((stations, count, comps * taps), jnp.bfloat16),
             jax.ShapeDtypeStruct((stations, count, LANES), jnp.float32),
             jax.ShapeDtypeStruct((stations * count * kept, LANES), jnp.float32),
         ),
-        in_specs=[smem, smem, hbm, hbm],
+        in_specs=[hbm] * 4,
         out_specs=(vmem, vmem, vmem, vmem, vmem),
         scratch_shapes=[pltpu.VMEM(wave.shape, wave.dtype), pltpu.VMEM(bank.shape, bank.dtype)]
         + scratch(2 * length)
-        + [pltpu.SemaphoreType.DMA((2,))],
+        + [pltpu.SemaphoreType.DMA((4,))],
         compiler_params=params,
         name="first_block",
     )(moveouts, mask, wave, bank)
     last = pl.pallas_call(
         functools.partial(last_block, taps=taps),
-        out_shape=jax.ShapeDtypeStruct((count, length), jnp.float32),
-        in_specs=[smem, smem, vmem, vmem, vmem, vmem, vmem],
+        out_shape=jax.ShapeDtypeStruct((count * rows, LANES), jnp.float32),
+        in_specs=[hbm] * 2 + [vmem] * 5,
         out_specs=vmem,
-        scratch_shapes=scratch(last_width),
+        scratch_shapes=scratch(last_width) + [pltpu.SemaphoreType.DMA((2,))],
         compiler_params=params,
         name="last_block",
     )(moveouts, mask, later, following, turned, scale, both)
 
     number = lax.axis_size("sta")
-    if number != 4:
-        first, last = lax.psum((first, last), "sta")
-        counts = first[:1, length:]
-        gain = [math.sqrt(comps * taps) * lax.rsqrt(counts[:, b : b + 1]) for b in range(blocks)]
-        return jnp.concatenate([first[:, :length] * gain[0], last * gain[1]], axis=1)
 
     def exchange(part, step):
         return lax.ppermute(part, "sta", [(k, k ^ step) for k in range(number)])
@@ -278,19 +289,25 @@
     def decode(part):
         return part.astype(jnp.float32) * (1.0 / WIRE_SCALE)
 
-    coded_last = code(last)
-    far_first = exchange(code(first), 2)
-    far = [exchange(coded_last, step) for step in (3, 2)]
-    first = first + decode(far_first)
-    near = exchange(jnp.concatenate([code(first), coded_last], axis=1), 1)
+    if number == 4:
+        far_first = exchange(code(first), 2)
+        coded_last = code(last)
+        far = [exchange(coded_last, step) for step in (3, 2, 1)]
+        first = first + decode(far_first)
+        near = decode(exchange(code(first), 1))
+        far = decode(far[0]) + decode(far[1]) + decode(far[2])
+    else:
+        first, last = lax.psum((first, last), "sta")
+        near, far = jnp.zeros_like(first), jnp.zeros_like(last)
     return pl.pallas_call(
         functools.partial(finish, factor=math.sqrt(comps * taps)),
         out_shape=jax.ShapeDtypeStruct((count, samples), jnp.float32),
         in_specs=[vmem] * 4,
         out_specs=vmem,
+        scratch_shapes=[pltpu.VMEM((count * rows, LANES), jnp.float32)],
         compiler_params=params,
         name="finish",
-    )(first, last, decode(near), decode(far[0]) + decode(far[1]))
+    )(first, near, last, far)
 
 
 def solution(mesh):

time: 21.6 us -> 20.3 us (0.940)
  waiting for transfers between devices: 5.3 us -> 3.97 us
  starting transfers between devices: 10 us -> 10.8 us
  Pallas kernels: 5.96 us -> 5.21 us
    ppermute x4 -> x5, waiting for transfers between devices: 5.3 us -> 3.97 us  [exchange(): return lax.ppermute(part, 'sta', [(k, k ^ step) for k in range(number)])]
    ppermute x4 -> x5, starting transfers between devices: 7.07 us -> 7.85 us  [exchange(): return lax.ppermute(part, 'sta', [(k, k ^ step) for k in range(number)])]
    pallas_call x1, Pallas kernels: 3.24 us -> 2.75 us  [shards(): pl.pallas_call(first_block, out_shape=(jax.ShapeDtypeStruct((count * rows...]
    pallas_call x1, Pallas kernels: 1.91 us -> 1.59 us  [shards(): pl.pallas_call(functools.partial(last_block, taps=taps), out_shape=jax.Sh...]
  transfers between devices with their start and end apart: 5 -> 6, of which waited for: 2 -> 2; matrix products, arithmetic and copies ran while one was open for 1% -> 1% of each run, Pallas kernels for 24% -> 22%
where the time goes in v3:
time: 20.3 us; the launch traced here: 20.2 us
  starting transfers between devices  10.8 us (53%)
  Pallas kernels  5.21 us (26%)
  waiting for transfers between devices  3.97 us (20%)
    ppermute x5, starting transfers between devices, exchange(): return lax.ppermute(part, 'sta', [(k, k ^ step) for k in range(number)])  7.85 us
    ppermute x5, waiting for transfers between devices, exchange(): return lax.ppermute(part, 'sta', [(k, k ^ step) for k in range(number)])  3.97 us
    ppermute x1, starting transfers between devices, from_next(): lax.ppermute(value, axis, [(k, (k - 1) % count) for k in range(count)])  2.94 us
    pallas_call x1, Pallas kernels, shards(): pl.pallas_call(first_block, out_shape=(jax.ShapeDtypeStruct((count * rows...  2.75 us
    pallas_call x1, Pallas kernels, shards(): pl.pallas_call(functools.partial(last_block, taps=taps), out_shape=jax.Sh...  1.59 us
    pallas_call x1, Pallas kernels, shards(): pl.pallas_call(functools.partial(finish, factor=math.sqrt(comps * taps)),...  0.87 us
  transfers between devices with their start and end apart: 6, of which 2 were waited for; matrix products, arithmetic and copies ran while one was open for 1% of the time, Pallas kernels for 22%

profile of v3, /device:TPU:0, one launch (start us, length us, event | category | flops | bytes accessed | tf_op | source)
XLA Modules:
  0.0 20.2 jit_solution(13107277701512981912)
XLA Ops:
  0.0 0.0 copy-start.1
  0.0 0.0 copy-start
  0.0 2.9 %collective-permute-start.2 = (bf16[3,2,2048]{2,1,0:T(2,128)(2,1)}, bf16[3,2,2048]{2,1,0:T(2,128)(2,1)S(1)}, u32[]{:S(2)}, u32[]{:S(2)}) collective-permute-start(bf16[3,2,2048]{2,1,0:T(2,128)(2,1)} %bitcast.3), channel_id=1, source_target_pairs={{0,2},{2,0},{1,3},{3,1},{4,6},{6,4},{5,7},{7,5},{8,10},{10,8},{9,1... | collective-permute-start | bytes 73736 | tf_op jit(solution)/shard_map/ppermute | solution.py:22
  2.9 0.0 copy-done.1
  2.9 0.0 copy-done
  2.9 2.8 %first_block.1 = (f32[264,128]{1,0:T(8,128)S(1)}, bf16[3,2,512]{2,1,0:T(2,128)(2,1)S(1)}, bf16[2,32,1200]{2,1,0:T(8,128)(2,1)S(1)}, f32[2,32,128]{2,1,0:T(8,128)S(1)}, f32[256,128]{1,0:T(8,128)S(1)}) custom-call(s32[2,32]{1,0:T(2,128)S(1)} %copy-done, s32[2,2]{1,0:T(2,128)S(1)} %copy-done.1, bf16[3,2,2048]{2,1,0:T(2,128)(2,1)} %bitcast.4, ...), custom_call_target="tpu_custom_call" | custom-call | tf_op jit(solution)/shard_map/first_block/pallas_call | solution.py:254
  5.7 2.7 %collective-permute-start = (f16[264,128]{1,0:T(8,128)(2,1)S(1)}, f16[264,128]{1,0:T(8,128)(2,1)S(1)}, u32[]{:S(2)}, u32[]{:S(2)}) collective-permute-start(f16[264,128]{1,0:T(8,128)(2,1)S(1)} %multiply_convert_fusion.1), channel_id=1, source_target_pairs={{0,8},{4,12},{8,0},{12,4},{1,9},{5,13},{9,1},{13,5},{2,10},{6,14},... | collective-permute-start | bytes 202760 | tf_op jit(solution)/shard_map/ppermute | solution.py:284
  8.4 0.0 collective-permute-done.2
  8.4 1.6 %last_block.1.last_ref = f32[256,128]{1,0:T(8,128)S(1)} custom-call(s32[2,32]{1,0:T(2,128)S(1)} %copy-done, s32[2,2]{1,0:T(2,128)S(1)} %copy-done.1, bf16[3,2,512]{2,1,0:T(2,128)(2,1)S(1)} %get-tuple-element.11.later_ref, bf16[3,2,2048]{2,1,0:T(2,128)(2,1)S(1)} %broadcast_select_fusion.next_ref, bf16[2,32,1200]{2,1,0:T(8,128)(2,1)S(1)} %get-tuple-element.12.turned_ref, ...), custom_call_target="tpu_custom_call" | custom-call | tf_op jit(solution)/shard_map/last_block/pallas_call | solution.py:271
  10.1 1.6 %collective-permute-start.5 = (f16[256,128]{1,0:T(8,128)(2,1)S(1)}, f16[256,128]{1,0:T(8,128)(2,1)S(1)}, u32[]{:S(2)}, u32[]{:S(2)}) collective-permute-start(f16[256,128]{1,0:T(8,128)(2,1)S(1)} %multiply_convert_fusion.2), channel_id=1, source_target_pairs={{0,4},{4,0},{8,12},{12,8},{1,5},{5,1},{9,13},{13,9},{2,6},{6,2},{1... | collective-permute-start | bytes 196616 | tf_op jit(solution)/shard_map/ppermute | solution.py:284
  11.7 0.3 %collective-permute-start.4 = (f16[256,128]{1,0:T(8,128)(2,1)S(1)}, f16[256,128]{1,0:T(8,128)(2,1)S(1)}, u32[]{:S(2)}, u32[]{:S(2)}) collective-permute-start(f16[256,128]{1,0:T(8,128)(2,1)S(1)} %multiply_convert_fusion.2), channel_id=1, source_target_pairs={{0,8},{4,12},{8,0},{12,4},{1,9},{5,13},{9,1},{13,5},{2,10},{6,14},... | collective-permute-start | bytes 196616 | tf_op jit(solution)/shard_map/ppermute | solution.py:284
  12.0 2.5 %collective-permute-start.3 = (f16[256,128]{1,0:T(8,128)(2,1)S(1)}, f16[256,128]{1,0:T(8,128)(2,1)S(1)}, u32[]{:S(2)}, u32[]{:S(2)}) collective-permute-start(f16[256,128]{1,0:T(8,128)(2,1)S(1)} %multiply_convert_fusion.2), channel_id=1, source_target_pairs={{0,12},{4,8},{8,4},{12,0},{1,13},{5,9},{9,5},{13,1},{2,14},{6,10},... | collective-permute-start | bytes 196616 | tf_op jit(solution)/shard_map/ppermute | solution.py:284
  14.5 0.0 collective-permute-done
  14.5 0.7 %collective-permute-start.1 = (f16[264,128]{1,0:T(8,128)(2,1)S(1)}, f16[264,128]{1,0:T(8,128)(2,1)S(1)}, u32[]{:S(2)}, u32[]{:S(2)}) collective-permute-start(f16[264,128]{1,0:T(8,128)(2,1)S(1)} %get-tuple-element.15), channel_id=1, source_target_pairs={{0,4},{4,0},{8,12},{12,8},{1,5},{5,1},{9,13},{13,9},{2,6},{6,2},{1... | collective-permute-start | bytes 202760 | tf_op jit(solution)/shard_map/ppermute | solution.py:284
  15.3 0.0 collective-permute-done.5
  15.3 3.7 %collective-permute-done.4 = f16[256,128]{1,0:T(8,128)(2,1)S(1)} collective-permute-done((f16[256,128]{1,0:T(8,128)(2,1)S(1)}, f16[256,128]{1,0:T(8,128)(2,1)S(1)}, u32[]{:S(2)}, u32[]{:S(2)}) %collective-permute-start.4) | collective-permute-done | bytes 65568 | tf_op jit(solution)/shard_map/ppermute | solution.py:284
  19.0 0.0 collective-permute-done.3
  19.0 0.3 %collective-permute-done.1 = f16[264,128]{1,0:T(8,128)(2,1)S(1)} collective-permute-done((f16[264,128]{1,0:T(8,128)(2,1)S(1)}, f16[264,128]{1,0:T(8,128)(2,1)S(1)}, u32[]{:S(2)}, u32[]{:S(2)}) %collective-permute-start.1) | collective-permute-done | bytes 67616 | tf_op jit(solution)/shard_map/ppermute | solution.py:284
  19.3 0.9 %finish.1 = f32[32,2048]{1,0:T(8,128)} custom-call(f32[264,128]{1,0:T(8,128)S(1)} %get-tuple-element.16.first_ref, f32[264,128]{1,0:T(8,128)S(1)} %convert_multiply_fusion.near_ref, f32[256,128]{1,0:T(8,128)S(1)} %last_block.1.last_ref, f32[256,128]{1,0:T(8,128)S(1)} %add_multiply_fusion.far_ref), custom_call_target="tpu_custom_call" | custom-call | tf_op jit(solution)/shard_map/finish/pallas_call | solution.py:302
  (6 shorter events, 0.1 us)
Async XLA Ops:
  0.0 2.9 %copy-start.1 = (s32[2,2]{1,0:T(2,128)S(1)}, s32[2,2]{1,0:T(2,128)}, u32[]{:S(2)}) copy-start(s32[2,2]{1,0:T(2,128)} %flags_hbm.3) | copy-start | bytes 52
  0.0 2.9 %copy-start = (s32[2,32]{1,0:T(2,128)S(1)}, s32[2,32]{1,0:T(2,128)}, u32[]{:S(2)}) copy-start(s32[2,32]{1,0:T(2,128)} %moves_hbm.3) | copy-start | bytes 772
  0.0 8.4 %collective-permute-start.2 = (bf16[3,2,2048]{2,1,0:T(2,128)(2,1)}, bf16[3,2,2048]{2,1,0:T(2,128)(2,1)S(1)}, u32[]{:S(2)}, u32[]{:S(2)}) collective-permute-start(bf16[3,2,2048]{2,1,0:T(2,128)(2,1)} %bitcast.3), channel_id=1, source_target_pairs={{0,2},{2,0},{1,3},{3,1},{4,6},{6,4},{5,7},{7,5},{8,10},{10,8},{9,1... | collective-permute-start | bytes 73736 | tf_op jit(solution)/shard_map/ppermute | solution.py:22
  5.7 8.8 %collective-permute-start = (f16[264,128]{1,0:T(8,128)(2,1)S(1)}, f16[264,128]{1,0:T(8,128)(2,1)S(1)}, u32[]{:S(2)}, u32[]{:S(2)}) collective-permute-start(f16[264,128]{1,0:T(8,128)(2,1)S(1)} %multiply_convert_fusion.1), channel_id=1, source_target_pairs={{0,8},{4,12},{8,0},{12,4},{1,9},{5,13},{9,1},{13,5},{2,10},{6,14},... | collective-permute-start | bytes 202760 | tf_op jit(solution)/shard_map/ppermute | solution.py:284
  10.1 5.2 %collective-permute-start.5 = (f16[256,128]{1,0:T(8,128)(2,1)S(1)}, f16[256,128]{1,0:T(8,128)(2,1)S(1)}, u32[]{:S(2)}, u32[]{:S(2)}) collective-permute-start(f16[256,128]{1,0:T(8,128)(2,1)S(1)} %multiply_convert_fusion.2), channel_id=1, source_target_pairs={{0,4},{4,0},{8,12},{12,8},{1,5},{5,1},{9,13},{13,9},{2,6},{6,2},{1... | collective-permute-start | bytes 196616 | tf_op jit(solution)/shard_map/ppermute | solution.py:284
  11.7 7.3 %collective-permute-start.4 = (f16[256,128]{1,0:T(8,128)(2,1)S(1)}, f16[256,128]{1,0:T(8,128)(2,1)S(1)}, u32[]{:S(2)}, u32[]{:S(2)}) collective-permute-start(f16[256,128]{1,0:T(8,128)(2,1)S(1)} %multiply_convert_fusion.2), channel_id=1, source_target_pairs={{0,8},{4,12},{8,0},{12,4},{1,9},{5,13},{9,1},{13,5},{2,10},{6,14},... | collective-permute-start | bytes 196616 | tf_op jit(solution)/shard_map/ppermute | solution.py:284
  12.0 6.9 %collective-permute-start.3 = (f16[256,128]{1,0:T(8,128)(2,1)S(1)}, f16[256,128]{1,0:T(8,128)(2,1)S(1)}, u32[]{:S(2)}, u32[]{:S(2)}) collective-permute-start(f16[256,128]{1,0:T(8,128)(2,1)S(1)} %multiply_convert_fusion.2), channel_id=1, source_target_pairs={{0,12},{4,8},{8,4},{12,0},{1,13},{5,9},{9,5},{13,1},{2,14},{6,10},... | collective-permute-start | bytes 196616 | tf_op jit(solution)/shard_map/ppermute | solution.py:284
  14.5 4.7 %collective-permute-start.1 = (f16[264,128]{1,0:T(8,128)(2,1)S(1)}, f16[264,128]{1,0:T(8,128)(2,1)S(1)}, u32[]{:S(2)}, u32[]{:S(2)}) collective-permute-start(f16[264,128]{1,0:T(8,128)(2,1)S(1)} %get-tuple-element.15), channel_id=1, source_target_pairs={{0,4},{4,0},{8,12},{12,8},{1,5},{5,1},{9,13},{13,9},{2,6},{6,2},{1... | collective-permute-start | bytes 202760 | tf_op jit(solution)/shard_map/ppermute | solution.py:284

commit v4 on v3

--- a/solution.py
+++ b/solution.py
@@ -14,6 +14,7 @@
 LANES = 128
 GROUP = 16
 COUNT_ROWS = 8
+TILES = 4
 WIRE_SCALE = 2.0**13
 
 
@@ -91,22 +92,22 @@
     stations, count, depth = turned_ref.shape
     whole = taps // LANES
     tail = taps - whole * LANES
-    span = tiles * LANES
     for s in range(stations):
-        pieces = []
-        for c in range(comps):
-            top = (s * comps + c) * LANES
-            for q in range(whole):
-                pieces.append(hankel[top : top + LANES, q * LANES : q * LANES + span])
-        for c in range(comps):
-            top = (s * comps + c) * LANES
-            pieces.append(hankel[top : top + tail, whole * LANES : whole * LANES + span])
-        product = jnp.dot(turned_ref[s], jnp.concatenate(pieces, axis=0), preferred_element_type=jnp.float32)
-        product = product * inverse[s : s + 1, :span]
-        for x in range(tiles):
-            for g in range(0, count, 8):
-                tile = product[g : g + 8, x * LANES : (x + 1) * LANES] * scale_ref[s, g : g + 8, :]
-                put(s * count + g, x, tile)
+        tops = [(s * comps + c) * LANES for c in range(comps)]
+        for first in range(0, tiles, TILES):
+            size = min(TILES, tiles - first)
+
+            def part(top, rows, q):
+                return hankel[top : top + rows, (first + q) * LANES : (first + q + size) * LANES]
+
+            pieces = [part(top, LANES, q) for top in tops for q in range(whole)]
+            pieces += [part(top, tail, whole) for top in tops]
+            product = jnp.dot(turned_ref[s], jnp.concatenate(pieces, axis=0), preferred_element_type=jnp.float32)
+            product = product * inverse[s : s + 1, first * LANES : (first + size) * LANES]
+            for x in range(size):
+                for g in range(0, count, 8):
+                    tile = product[g : g + 8, x * LANES : (x + 1) * LANES] * scale_ref[s, g : g + 8, :]
+                    put(s * count + g, first + x, tile)
 
 
 def align(moves, flags, block, aligned, out_ref, rows):
@@ -222,6 +223,10 @@
             left = (b * rows + x) * LANES
             for g in range(0, count, 8):
                 out_ref[g : g + 8, left : left + LANES] = sums[pl.ds(g * rows + x, 8, stride=rows), :]
+
+
+def in_hbm(value):
+    return pltpu.with_memory_space_constraint(value, pltpu.HBM)
 
 
 def shards(data, templates, moveouts, mask):
@@ -267,7 +272,7 @@
         + [pltpu.SemaphoreType.DMA((4,))],
         compiler_params=params,
         name="first_block",
-    )(moveouts, mask, wave, bank)
+    )(in_hbm(moveouts), in_hbm(mask), wave, bank)
     last = pl.pallas_call(
         functools.partial(last_block, taps=taps),
         out_shape=jax.ShapeDtypeStruct((count * rows, LANES), jnp.float32),
@@ -276,7 +281,7 @@
         scratch_shapes=scratch(last_width) + [pltpu.SemaphoreType.DMA((2,))],
         compiler_params=params,
         name="last_block",
-    )(moveouts, mask, later, following, turned, scale, both)
+    )(in_hbm(moveouts), in_hbm(mask), later, following, turned, scale, both)
 
     number = lax.axis_size("sta")
 

time: 20.3 us -> 20.1 us (level)
  Pallas kernels: 5.21 us -> 4.99 us
    pallas_call x1, Pallas kernels: 1.59 us -> 1.37 us  [shards(): pl.pallas_call(functools.partial(last_block, taps=taps), out_shape=jax.Sh...]
  transfers between devices with their start and end apart: 6 -> 6, of which waited for: 2 -> 2; matrix products, arithmetic and copies ran while one was open for 1% -> 1% of each run, Pallas kernels for 22% -> 21%
where the time goes in v4:
time: 20.1 us; the launch traced here: 20 us
  starting transfers between devices  10.8 us (54%)
  Pallas kernels  4.99 us (25%)
  waiting for transfers between devices  3.97 us (20%)
    ppermute x5, starting transfers between devices, exchange(): return lax.ppermute(part, 'sta', [(k, k ^ step) for k in range(number)])  7.85 us
    ppermute x5, waiting for transfers between devices, exchange(): return lax.ppermute(part, 'sta', [(k, k ^ step) for k in range(number)])  3.97 us
    ppermute x1, starting transfers between devices, from_next(): lax.ppermute(value, axis, [(k, (k - 1) % count) for k in range(count)])  2.94 us
    pallas_call x1, Pallas kernels, shards(): pl.pallas_call(first_block, out_shape=(jax.ShapeDtypeStruct((count * rows...  2.75 us
    pallas_call x1, Pallas kernels, shards(): pl.pallas_call(functools.partial(last_block, taps=taps), out_shape=jax.Sh...  1.37 us
    pallas_call x1, Pallas kernels, shards(): pl.pallas_call(functools.partial(finish, factor=math.sqrt(comps * taps)),...  0.87 us
  transfers between devices with their start and end apart: 6, of which 2 were waited for; matrix products, arithmetic and copies ran while one was open for 1% of the time, Pallas kernels for 21%

profile of v4, /device:TPU:0, one launch (start us, length us, event | category | flops | bytes accessed | tf_op | source)
XLA Modules:
  0.0 20.0 jit_solution(11312177757660613090)
XLA Ops:
  0.0 2.9 %collective-permute-start.2 = (bf16[3,2,2048]{2,1,0:T(2,128)(2,1)}, bf16[3,2,2048]{2,1,0:T(2,128)(2,1)S(1)}, u32[]{:S(2)}, u32[]{:S(2)}) collective-permute-start(bf16[3,2,2048]{2,1,0:T(2,128)(2,1)} %bitcast.3), channel_id=1, source_target_pairs={{0,2},{2,0},{1,3},{3,1},{4,6},{6,4},{5,7},{7,5},{8,10},{10,8},{9,1... | collective-permute-start | bytes 73736 | tf_op jit(solution)/shard_map/ppermute | solution.py:23
  2.9 2.8 %first_block.1 = (f32[264,128]{1,0:T(8,128)S(1)}, bf16[3,2,512]{2,1,0:T(2,128)(2,1)S(1)}, bf16[2,32,1200]{2,1,0:T(8,128)(2,1)S(1)}, f32[2,32,128]{2,1,0:T(8,128)S(1)}, f32[256,128]{1,0:T(8,128)S(1)}) custom-call(s32[2,32]{1,0:T(2,128)} %moves_hbm.3, s32[2,2]{1,0:T(2,128)} %flags_hbm.3, bf16[3,2,2048]{2,1,0:T(2,128)(2,1)} %bitcast.4, ...), custom_call_target="tpu_custom_call" | custom-call | tf_op jit(solution)/shard_map/first_block/pallas_call | solution.py:259
  5.7 2.7 %collective-permute-start = (f16[264,128]{1,0:T(8,128)(2,1)S(1)}, f16[264,128]{1,0:T(8,128)(2,1)S(1)}, u32[]{:S(2)}, u32[]{:S(2)}) collective-permute-start(f16[264,128]{1,0:T(8,128)(2,1)S(1)} %multiply_convert_fusion.1), channel_id=1, source_target_pairs={{0,8},{4,12},{8,0},{12,4},{1,9},{5,13},{9,1},{13,5},{2,10},{6,14},... | collective-permute-start | bytes 202760 | tf_op jit(solution)/shard_map/ppermute | solution.py:289
  8.4 0.0 collective-permute-done.2
  8.4 1.4 %last_block.1.last_ref = f32[256,128]{1,0:T(8,128)S(1)} custom-call(s32[2,32]{1,0:T(2,128)} %moves_hbm.3, s32[2,2]{1,0:T(2,128)} %flags_hbm.3, bf16[3,2,512]{2,1,0:T(2,128)(2,1)S(1)} %get-tuple-element.11.later_ref, bf16[3,2,2048]{2,1,0:T(2,128)(2,1)S(1)} %broadcast_select_fusion.next_ref, bf16[2,32,1200]{2,1,0:T(8,128)(2,1)S(1)} %get-tuple-element.12.turned_ref, ...), custom_call_target="tpu_custom_call" | custom-call | tf_op jit(solution)/shard_map/last_block/pallas_call | solution.py:276
  9.8 1.6 %collective-permute-start.5 = (f16[256,128]{1,0:T(8,128)(2,1)S(1)}, f16[256,128]{1,0:T(8,128)(2,1)S(1)}, u32[]{:S(2)}, u32[]{:S(2)}) collective-permute-start(f16[256,128]{1,0:T(8,128)(2,1)S(1)} %multiply_convert_fusion.2), channel_id=1, source_target_pairs={{0,4},{4,0},{8,12},{12,8},{1,5},{5,1},{9,13},{13,9},{2,6},{6,2},{1... | collective-permute-start | bytes 196616 | tf_op jit(solution)/shard_map/ppermute | solution.py:289
  11.5 0.3 %collective-permute-start.4 = (f16[256,128]{1,0:T(8,128)(2,1)S(1)}, f16[256,128]{1,0:T(8,128)(2,1)S(1)}, u32[]{:S(2)}, u32[]{:S(2)}) collective-permute-start(f16[256,128]{1,0:T(8,128)(2,1)S(1)} %multiply_convert_fusion.2), channel_id=1, source_target_pairs={{0,8},{4,12},{8,0},{12,4},{1,9},{5,13},{9,1},{13,5},{2,10},{6,14},... | collective-permute-start | bytes 196616 | tf_op jit(solution)/shard_map/ppermute | solution.py:289
  11.8 2.5 %collective-permute-start.3 = (f16[256,128]{1,0:T(8,128)(2,1)S(1)}, f16[256,128]{1,0:T(8,128)(2,1)S(1)}, u32[]{:S(2)}, u32[]{:S(2)}) collective-permute-start(f16[256,128]{1,0:T(8,128)(2,1)S(1)} %multiply_convert_fusion.2), channel_id=1, source_target_pairs={{0,12},{4,8},{8,4},{12,0},{1,13},{5,9},{9,5},{13,1},{2,14},{6,10},... | collective-permute-start | bytes 196616 | tf_op jit(solution)/shard_map/ppermute | solution.py:289
  14.3 0.0 collective-permute-done
  14.3 0.7 %collective-permute-start.1 = (f16[264,128]{1,0:T(8,128)(2,1)S(1)}, f16[264,128]{1,0:T(8,128)(2,1)S(1)}, u32[]{:S(2)}, u32[]{:S(2)}) collective-permute-start(f16[264,128]{1,0:T(8,128)(2,1)S(1)} %get-tuple-element.15), channel_id=1, source_target_pairs={{0,4},{4,0},{8,12},{12,8},{1,5},{5,1},{9,13},{13,9},{2,6},{6,2},{1... | collective-permute-start | bytes 202760 | tf_op jit(solution)/shard_map/ppermute | solution.py:289
  15.1 0.0 collective-permute-done.5
  15.1 3.7 %collective-permute-done.4 = f16[256,128]{1,0:T(8,128)(2,1)S(1)} collective-permute-done((f16[256,128]{1,0:T(8,128)(2,1)S(1)}, f16[256,128]{1,0:T(8,128)(2,1)S(1)}, u32[]{:S(2)}, u32[]{:S(2)}) %collective-permute-start.4) | collective-permute-done | bytes 65568 | tf_op jit(solution)/shard_map/ppermute | solution.py:289
  18.7 0.0 collective-permute-done.3
  18.8 0.3 %collective-permute-done.1 = f16[264,128]{1,0:T(8,128)(2,1)S(1)} collective-permute-done((f16[264,128]{1,0:T(8,128)(2,1)S(1)}, f16[264,128]{1,0:T(8,128)(2,1)S(1)}, u32[]{:S(2)}, u32[]{:S(2)}) %collective-permute-start.1) | collective-permute-done | bytes 67616 | tf_op jit(solution)/shard_map/ppermute | solution.py:289
  19.1 0.9 %finish.1 = f32[32,2048]{1,0:T(8,128)} custom-call(f32[264,128]{1,0:T(8,128)S(1)} %get-tuple-element.16.first_ref, f32[264,128]{1,0:T(8,128)S(1)} %convert_multiply_fusion.near_ref, f32[256,128]{1,0:T(8,128)S(1)} %last_block.1.last_ref, f32[256,128]{1,0:T(8,128)S(1)} %add_multiply_fusion.far_ref), custom_call_target="tpu_custom_call" | custom-call | tf_op jit(solution)/shard_map/finish/pallas_call | solution.py:307
  (6 shorter events, 0.1 us)
Async XLA Ops:
  0.0 8.4 %collective-permute-start.2 = (bf16[3,2,2048]{2,1,0:T(2,128)(2,1)}, bf16[3,2,2048]{2,1,0:T(2,128)(2,1)S(1)}, u32[]{:S(2)}, u32[]{:S(2)}) collective-permute-start(bf16[3,2,2048]{2,1,0:T(2,128)(2,1)} %bitcast.3), channel_id=1, source_target_pairs={{0,2},{2,0},{1,3},{3,1},{4,6},{6,4},{5,7},{7,5},{8,10},{10,8},{9,1... | collective-permute-start | bytes 73736 | tf_op jit(solution)/shard_map/ppermute | solution.py:23
  5.7 8.6 %collective-permute-start = (f16[264,128]{1,0:T(8,128)(2,1)S(1)}, f16[264,128]{1,0:T(8,128)(2,1)S(1)}, u32[]{:S(2)}, u32[]{:S(2)}) collective-permute-start(f16[264,128]{1,0:T(8,128)(2,1)S(1)} %multiply_convert_fusion.1), channel_id=1, source_target_pairs={{0,8},{4,12},{8,0},{12,4},{1,9},{5,13},{9,1},{13,5},{2,10},{6,14},... | collective-permute-start | bytes 202760 | tf_op jit(solution)/shard_map/ppermute | solution.py:289
  9.8 5.2 %collective-permute-start.5 = (f16[256,128]{1,0:T(8,128)(2,1)S(1)}, f16[256,128]{1,0:T(8,128)(2,1)S(1)}, u32[]{:S(2)}, u32[]{:S(2)}) collective-permute-start(f16[256,128]{1,0:T(8,128)(2,1)S(1)} %multiply_convert_fusion.2), channel_id=1, source_target_pairs={{0,4},{4,0},{8,12},{12,8},{1,5},{5,1},{9,13},{13,9},{2,6},{6,2},{1... | collective-permute-start | bytes 196616 | tf_op jit(solution)/shard_map/ppermute | solution.py:289
  11.5 7.3 %collective-permute-start.4 = (f16[256,128]{1,0:T(8,128)(2,1)S(1)}, f16[256,128]{1,0:T(8,128)(2,1)S(1)}, u32[]{:S(2)}, u32[]{:S(2)}) collective-permute-start(f16[256,128]{1,0:T(8,128)(2,1)S(1)} %multiply_convert_fusion.2), channel_id=1, source_target_pairs={{0,8},{4,12},{8,0},{12,4},{1,9},{5,13},{9,1},{13,5},{2,10},{6,14},... | collective-permute-start | bytes 196616 | tf_op jit(solution)/shard_map/ppermute | solution.py:289
  11.8 6.9 %collective-permute-start.3 = (f16[256,128]{1,0:T(8,128)(2,1)S(1)}, f16[256,128]{1,0:T(8,128)(2,1)S(1)}, u32[]{:S(2)}, u32[]{:S(2)}) collective-permute-start(f16[256,128]{1,0:T(8,128)(2,1)S(1)} %multiply_convert_fusion.2), channel_id=1, source_target_pairs={{0,12},{4,8},{8,4},{12,0},{1,13},{5,9},{9,5},{13,1},{2,14},{6,10},... | collective-permute-start | bytes 196616 | tf_op jit(solution)/shard_map/ppermute | solution.py:289
  14.3 4.7 %collective-permute-start.1 = (f16[264,128]{1,0:T(8,128)(2,1)S(1)}, f16[264,128]{1,0:T(8,128)(2,1)S(1)}, u32[]{:S(2)}, u32[]{:S(2)}) collective-permute-start(f16[264,128]{1,0:T(8,128)(2,1)S(1)} %get-tuple-element.15), channel_id=1, source_target_pairs={{0,4},{4,0},{8,12},{12,8},{1,5},{5,1},{9,13},{13,9},{2,6},{6,2},{1... | collective-permute-start | bytes 202760 | tf_op jit(solution)/shard_map/ppermute | solution.py:289

commit v5 on v4

--- a/solution.py
+++ b/solution.py
@@ -136,6 +136,11 @@
     out_ref[top : top + COUNT_ROWS, :] = counts
 
 
+def by_part(source, target):
+    stations, comps = target.shape[:2]
+    return tuple((source.at[s, c], target.at[s, c]) for s in range(stations) for c in range(comps))
+
+
 def fetch(pairs, ready):
     copies = [pltpu.make_async_copy(source, target, ready.at[n]) for n, (source, target) in enumerate(pairs)]
     for copy in copies:
@@ -153,7 +158,7 @@
     length = rows * LANES
     pitch = aligned.shape[0] // (stations * count)
     kept = kept_ref.shape[0] // (stations * count)
-    copies = fetch(((wave_hbm, wave_ref), (bank_hbm, bank_ref), (moves_hbm, moves), (flags_hbm, flags)), ready)
+    copies = fetch((*by_part(bank_hbm, bank_ref), (wave_hbm, wave_ref), (moves_hbm, moves), (flags_hbm, flags)), ready)
     for copy in copies:
         copy.wait()
     put_counts(flags, out_ref, count * rows)
@@ -269,7 +274,7 @@
         out_specs=(vmem, vmem, vmem, vmem, vmem),
         scratch_shapes=[pltpu.VMEM(wave.shape, wave.dtype), pltpu.VMEM(bank.shape, bank.dtype)]
         + scratch(2 * length)
-        + [pltpu.SemaphoreType.DMA((4,))],
+        + [pltpu.SemaphoreType.DMA((stations * comps + 3,))],
         compiler_params=params,
         name="first_block",
     )(in_hbm(moveouts), in_hbm(mask), wave, bank)
@@ -297,7 +302,7 @@
     if number == 4:
         far_first = exchange(code(first), 2)
         coded_last = code(last)
-        far = [exchange(coded_last, step) for step in (3, 2, 1)]
+        far = [exchange(coded_last, step) for step in (2, 1, 3)]
         first = first + decode(far_first)
         near = decode(exchange(code(first), 1))
         far = decode(far[0]) + decode(far[1]) + decode(far[2])

time: 20.1 us -> 19.7 us (0.980)
  waiting for transfers between devices: 3.97 us -> 3.58 us
    ppermute x5, waiting for transfers between devices: 3.97 us -> 3.57 us  [exchange(): return lax.ppermute(part, 'sta', [(k, k ^ step) for k in range(number)])]
  transfers between devices with their start and end apart: 6 -> 6, of which waited for: 2 -> 3; matrix products, arithmetic and copies ran while one was open for 1% -> 1% of each run, Pallas kernels for 21% -> 21%
where the time goes in v5:
time: 19.7 us; the launch traced here: 19.5 us
  starting transfers between devices  10.8 us (55%)
  Pallas kernels  4.93 us (25%)
  waiting for transfers between devices  3.58 us (18%)
    ppermute x5, starting transfers between devices, exchange(): return lax.ppermute(part, 'sta', [(k, k ^ step) for k in range(number)])  7.86 us
    ppermute x5, waiting for transfers between devices, exchange(): return lax.ppermute(part, 'sta', [(k, k ^ step) for k in range(number)])  3.57 us
    ppermute x1, starting transfers between devices, from_next(): lax.ppermute(value, axis, [(k, (k - 1) % count) for k in range(count)])  2.94 us
    pallas_call x1, Pallas kernels, shards(): pl.pallas_call(first_block, out_shape=(jax.ShapeDtypeStruct((count * rows...  2.69 us
    pallas_call x1, Pallas kernels, shards(): pl.pallas_call(functools.partial(last_block, taps=taps), out_shape=jax.Sh...  1.37 us
    pallas_call x1, Pallas kernels, shards(): pl.pallas_call(functools.partial(finish, factor=math.sqrt(comps * taps)),...  0.87 us
  transfers between devices with their start and end apart: 6, of which 3 were waited for; matrix products, arithmetic and copies ran while one was open for 1% of the time, Pallas kernels for 21%

profile of v5, /device:TPU:0, one launch (start us, length us, event | category | flops | bytes accessed | tf_op | source)
XLA Modules:
  0.0 19.5 jit_solution(10560008209778991443)
XLA Ops:
  0.0 2.9 %collective-permute-start.2 = (bf16[3,2,2048]{2,1,0:T(2,128)(2,1)}, bf16[3,2,2048]{2,1,0:T(2,128)(2,1)S(1)}, u32[]{:S(2)}, u32[]{:S(2)}) collective-permute-start(bf16[3,2,2048]{2,1,0:T(2,128)(2,1)} %bitcast.3), channel_id=1, source_target_pairs={{0,2},{2,0},{1,3},{3,1},{4,6},{6,4},{5,7},{7,5},{8,10},{10,8},{9,1... | collective-permute-start | bytes 73736 | tf_op jit(solution)/shard_map/ppermute | solution.py:23
  2.9 2.7 %first_block.1 = (f32[264,128]{1,0:T(8,128)S(1)}, bf16[3,2,512]{2,1,0:T(2,128)(2,1)S(1)}, bf16[2,32,1200]{2,1,0:T(8,128)(2,1)S(1)}, f32[2,32,128]{2,1,0:T(8,128)S(1)}, f32[256,128]{1,0:T(8,128)S(1)}) custom-call(s32[2,32]{1,0:T(2,128)} %moves_hbm.3, s32[2,2]{1,0:T(2,128)} %flags_hbm.3, bf16[3,2,2048]{2,1,0:T(2,128)(2,1)} %bitcast.4, ...), custom_call_target="tpu_custom_call" | custom-call | tf_op jit(solution)/shard_map/first_block/pallas_call | solution.py:264
  5.7 2.7 %collective-permute-start = (f16[264,128]{1,0:T(8,128)(2,1)S(1)}, f16[264,128]{1,0:T(8,128)(2,1)S(1)}, u32[]{:S(2)}, u32[]{:S(2)}) collective-permute-start(f16[264,128]{1,0:T(8,128)(2,1)S(1)} %multiply_convert_fusion.1), channel_id=1, source_target_pairs={{0,8},{4,12},{8,0},{12,4},{1,9},{5,13},{9,1},{13,5},{2,10},{6,14},... | collective-permute-start | bytes 202760 | tf_op jit(solution)/shard_map/ppermute | solution.py:294
  8.3 0.0 collective-permute-done.2
  8.4 1.4 %last_block.1.last_ref = f32[256,128]{1,0:T(8,128)S(1)} custom-call(s32[2,32]{1,0:T(2,128)} %moves_hbm.3, s32[2,2]{1,0:T(2,128)} %flags_hbm.3, bf16[3,2,512]{2,1,0:T(2,128)(2,1)S(1)} %get-tuple-element.11.later_ref, bf16[3,2,2048]{2,1,0:T(2,128)(2,1)S(1)} %broadcast_select_fusion.next_ref, bf16[2,32,1200]{2,1,0:T(8,128)(2,1)S(1)} %get-tuple-element.12.turned_ref, ...), custom_call_target="tpu_custom_call" | custom-call | tf_op jit(solution)/shard_map/last_block/pallas_call | solution.py:281
  9.8 1.4 %collective-permute-start.5 = (f16[256,128]{1,0:T(8,128)(2,1)S(1)}, f16[256,128]{1,0:T(8,128)(2,1)S(1)}, u32[]{:S(2)}, u32[]{:S(2)}) collective-permute-start(f16[256,128]{1,0:T(8,128)(2,1)S(1)} %multiply_convert_fusion.2), channel_id=1, source_target_pairs={{0,12},{4,8},{8,4},{12,0},{1,13},{5,9},{9,5},{13,1},{2,14},{6,10},... | collective-permute-start | bytes 196616 | tf_op jit(solution)/shard_map/ppermute | solution.py:294
  11.2 0.3 %collective-permute-start.4 = (f16[256,128]{1,0:T(8,128)(2,1)S(1)}, f16[256,128]{1,0:T(8,128)(2,1)S(1)}, u32[]{:S(2)}, u32[]{:S(2)}) collective-permute-start(f16[256,128]{1,0:T(8,128)(2,1)S(1)} %multiply_convert_fusion.2), channel_id=1, source_target_pairs={{0,4},{4,0},{8,12},{12,8},{1,5},{5,1},{9,13},{13,9},{2,6},{6,2},{1... | collective-permute-start | bytes 196616 | tf_op jit(solution)/shard_map/ppermute | solution.py:294
  11.5 2.7 %collective-permute-start.3 = (f16[256,128]{1,0:T(8,128)(2,1)S(1)}, f16[256,128]{1,0:T(8,128)(2,1)S(1)}, u32[]{:S(2)}, u32[]{:S(2)}) collective-permute-start(f16[256,128]{1,0:T(8,128)(2,1)S(1)} %multiply_convert_fusion.2), channel_id=1, source_target_pairs={{0,8},{4,12},{8,0},{12,4},{1,9},{5,13},{9,1},{13,5},{2,10},{6,14},... | collective-permute-start | bytes 196616 | tf_op jit(solution)/shard_map/ppermute | solution.py:294
  14.2 0.0 collective-permute-done
  14.3 0.8 %collective-permute-start.1 = (f16[264,128]{1,0:T(8,128)(2,1)S(1)}, f16[264,128]{1,0:T(8,128)(2,1)S(1)}, u32[]{:S(2)}, u32[]{:S(2)}) collective-permute-start(f16[264,128]{1,0:T(8,128)(2,1)S(1)} %get-tuple-element.15), channel_id=1, source_target_pairs={{0,4},{4,0},{8,12},{12,8},{1,5},{5,1},{9,13},{13,9},{2,6},{6,2},{1... | collective-permute-start | bytes 202760 | tf_op jit(solution)/shard_map/ppermute | solution.py:294
  15.0 1.7 %collective-permute-done.5 = f16[256,128]{1,0:T(8,128)(2,1)S(1)} collective-permute-done((f16[256,128]{1,0:T(8,128)(2,1)S(1)}, f16[256,128]{1,0:T(8,128)(2,1)S(1)}, u32[]{:S(2)}, u32[]{:S(2)}) %collective-permute-start.5) | collective-permute-done | bytes 65568 | tf_op jit(solution)/shard_map/ppermute | solution.py:294
  16.7 0.0 collective-permute-done.4
  16.7 1.1 %collective-permute-done.3 = f16[256,128]{1,0:T(8,128)(2,1)S(1)} collective-permute-done((f16[256,128]{1,0:T(8,128)(2,1)S(1)}, f16[256,128]{1,0:T(8,128)(2,1)S(1)}, u32[]{:S(2)}, u32[]{:S(2)}) %collective-permute-start.3) | collective-permute-done | bytes 65568 | tf_op jit(solution)/shard_map/ppermute | solution.py:294
  17.8 0.8 %collective-permute-done.1 = f16[264,128]{1,0:T(8,128)(2,1)S(1)} collective-permute-done((f16[264,128]{1,0:T(8,128)(2,1)S(1)}, f16[264,128]{1,0:T(8,128)(2,1)S(1)}, u32[]{:S(2)}, u32[]{:S(2)}) %collective-permute-start.1) | collective-permute-done | bytes 67616 | tf_op jit(solution)/shard_map/ppermute | solution.py:294
  18.6 0.9 %finish.1 = f32[32,2048]{1,0:T(8,128)} custom-call(f32[264,128]{1,0:T(8,128)S(1)} %get-tuple-element.16.first_ref, f32[264,128]{1,0:T(8,128)S(1)} %convert_multiply_fusion.near_ref, f32[256,128]{1,0:T(8,128)S(1)} %last_block.1.last_ref, f32[256,128]{1,0:T(8,128)S(1)} %add_multiply_fusion.far_ref), custom_call_target="tpu_custom_call" | custom-call | tf_op jit(solution)/shard_map/finish/pallas_call | solution.py:312
  (6 shorter events, 0.1 us)
Async XLA Ops:
  0.0 8.3 %collective-permute-start.2 = (bf16[3,2,2048]{2,1,0:T(2,128)(2,1)}, bf16[3,2,2048]{2,1,0:T(2,128)(2,1)S(1)}, u32[]{:S(2)}, u32[]{:S(2)}) collective-permute-start(bf16[3,2,2048]{2,1,0:T(2,128)(2,1)} %bitcast.3), channel_id=1, source_target_pairs={{0,2},{2,0},{1,3},{3,1},{4,6},{6,4},{5,7},{7,5},{8,10},{10,8},{9,1... | collective-permute-start | bytes 73736 | tf_op jit(solution)/shard_map/ppermute | solution.py:23
  5.7 8.6 %collective-permute-start = (f16[264,128]{1,0:T(8,128)(2,1)S(1)}, f16[264,128]{1,0:T(8,128)(2,1)S(1)}, u32[]{:S(2)}, u32[]{:S(2)}) collective-permute-start(f16[264,128]{1,0:T(8,128)(2,1)S(1)} %multiply_convert_fusion.1), channel_id=1, source_target_pairs={{0,8},{4,12},{8,0},{12,4},{1,9},{5,13},{9,1},{13,5},{2,10},{6,14},... | collective-permute-start | bytes 202760 | tf_op jit(solution)/shard_map/ppermute | solution.py:294
  9.8 6.9 %collective-permute-start.5 = (f16[256,128]{1,0:T(8,128)(2,1)S(1)}, f16[256,128]{1,0:T(8,128)(2,1)S(1)}, u32[]{:S(2)}, u32[]{:S(2)}) collective-permute-start(f16[256,128]{1,0:T(8,128)(2,1)S(1)} %multiply_convert_fusion.2), channel_id=1, source_target_pairs={{0,12},{4,8},{8,4},{12,0},{1,13},{5,9},{9,5},{13,1},{2,14},{6,10},... | collective-permute-start | bytes 196616 | tf_op jit(solution)/shard_map/ppermute | solution.py:294
  11.2 5.5 %collective-permute-start.4 = (f16[256,128]{1,0:T(8,128)(2,1)S(1)}, f16[256,128]{1,0:T(8,128)(2,1)S(1)}, u32[]{:S(2)}, u32[]{:S(2)}) collective-permute-start(f16[256,128]{1,0:T(8,128)(2,1)S(1)} %multiply_convert_fusion.2), channel_id=1, source_target_pairs={{0,4},{4,0},{8,12},{12,8},{1,5},{5,1},{9,13},{13,9},{2,6},{6,2},{1... | collective-permute-start | bytes 196616 | tf_op jit(solution)/shard_map/ppermute | solution.py:294
  11.5 6.3 %collective-permute-start.3 = (f16[256,128]{1,0:T(8,128)(2,1)S(1)}, f16[256,128]{1,0:T(8,128)(2,1)S(1)}, u32[]{:S(2)}, u32[]{:S(2)}) collective-permute-start(f16[256,128]{1,0:T(8,128)(2,1)S(1)} %multiply_convert_fusion.2), channel_id=1, source_target_pairs={{0,8},{4,12},{8,0},{12,4},{1,9},{5,13},{9,1},{13,5},{2,10},{6,14},... | collective-permute-start | bytes 196616 | tf_op jit(solution)/shard_map/ppermute | solution.py:294
  14.3 4.4 %collective-permute-start.1 = (f16[264,128]{1,0:T(8,128)(2,1)S(1)}, f16[264,128]{1,0:T(8,128)(2,1)S(1)}, u32[]{:S(2)}, u32[]{:S(2)}) collective-permute-start(f16[264,128]{1,0:T(8,128)(2,1)S(1)} %get-tuple-element.15), channel_id=1, source_target_pairs={{0,4},{4,0},{8,12},{12,8},{1,5},{5,1},{9,13},{13,9},{2,6},{6,2},{1... | collective-permute-start | bytes 202760 | tf_op jit(solution)/shard_map/ppermute | solution.py:294

commit v6 on v5

--- a/solution.py
+++ b/solution.py
@@ -21,7 +21,7 @@
 def from_next(value, axis):
     count = lax.axis_size(axis)
     arrived = lax.ppermute(value, axis, [(k, (k - 1) % count) for k in range(count)])
-    return jnp.where(lax.axis_index(axis) == count - 1, jnp.zeros_like(arrived), arrived)
+    return arrived
 
 
 def turn_groups(rows):
@@ -192,12 +192,16 @@
     pitch = aligned.shape[0] // (stations * count)
     kept = kept_ref.shape[0] // (stations * count)
     copies = fetch(((moves_hbm, moves), (flags_hbm, flags)), ready)
+    inside = jnp.where(lax.axis_index("tm") < lax.axis_size("tm") - 1, 1.0, 0.0).astype(next_ref.dtype)
+
+    def after(c, s):
+        return next_ref[c, s : s + 1, :length] * inside
 
     def window(s, c):
-        return jnp.concatenate([later_ref[c, s : s + 1, :], next_ref[c, s : s + 1, :length]], axis=1)
+        return jnp.concatenate([later_ref[c, s : s + 1, :], after(c, s)], axis=1)
 
     fill_hankel(window, hankel, stations, comps)
-    squares = [jnp.sum(part * part, axis=0) for part in (later_ref[...].astype(jnp.float32), next_ref[:, :, :length].astype(jnp.float32))]
+    squares = [jnp.sum(part * part, axis=0) for part in (later_ref[...].astype(jnp.float32), (next_ref[:, :, :length] * inside).astype(jnp.float32))]
     inverse = inverse_energy(jnp.concatenate(squares, axis=1), taps)
     for first in range(0, stations * count, 8):
         for x in range(kept):

time: 19.7 us -> 19.6 us (level)
  no operation moved by 1% of the time
where the time goes in v6:
time: 19.6 us; the launch traced here: 19.5 us
  starting transfers between devices  10.8 us (55%)
  Pallas kernels  4.92 us (25%)
  waiting for transfers between devices  3.57 us (18%)
    ppermute x5, starting transfers between devices, exchange(): return lax.ppermute(part, 'sta', [(k, k ^ step) for k in range(number)])  7.86 us
    ppermute x5, waiting for transfers between devices, exchange(): return lax.ppermute(part, 'sta', [(k, k ^ step) for k in range(number)])  3.57 us
    ppermute x1, starting transfers between devices, from_next(): lax.ppermute(value, axis, [(k, (k - 1) % count) for k in range(count)])  2.94 us
    pallas_call x1, Pallas kernels, shards(): pl.pallas_call(first_block, out_shape=(jax.ShapeDtypeStruct((count * rows...  2.69 us
    pallas_call x1, Pallas kernels, shards(): pl.pallas_call(functools.partial(last_block, taps=taps), out_shape=jax.Sh...  1.36 us
    pallas_call x1, Pallas kernels, shards(): pl.pallas_call(functools.partial(finish, factor=math.sqrt(comps * taps)),...  0.87 us
  transfers between devices with their start and end apart: 6, of which 3 were waited for; matrix products, arithmetic and copies ran while one was open for 1% of the time, Pallas kernels for 21%

profile of v6, /device:TPU:0, one launch (start us, length us, event | category | flops | bytes accessed | tf_op | source)
XLA Modules:
  0.0 19.5 jit_solution(5814016087470136868)
XLA Ops:
  0.0 2.9 %collective-permute-start.2 = (bf16[3,2,2048]{2,1,0:T(2,128)(2,1)}, bf16[3,2,2048]{2,1,0:T(2,128)(2,1)S(1)}, u32[]{:S(2)}, u32[]{:S(2)}) collective-permute-start(bf16[3,2,2048]{2,1,0:T(2,128)(2,1)} %bitcast.3), channel_id=1, source_target_pairs={{0,2},{2,0},{1,3},{3,1},{4,6},{6,4},{5,7},{7,5},{8,10},{10,8},{9,1... | collective-permute-start | bytes 73736 | tf_op jit(solution)/shard_map/ppermute | solution.py:23
  2.9 2.7 %first_block.1 = (f32[264,128]{1,0:T(8,128)S(1)}, bf16[3,2,512]{2,1,0:T(2,128)(2,1)S(1)}, bf16[2,32,1200]{2,1,0:T(8,128)(2,1)S(1)}, f32[2,32,128]{2,1,0:T(8,128)S(1)}, f32[256,128]{1,0:T(8,128)S(1)}) custom-call(s32[2,32]{1,0:T(2,128)} %moves_hbm.3, s32[2,2]{1,0:T(2,128)} %flags_hbm.3, bf16[3,2,2048]{2,1,0:T(2,128)(2,1)} %bitcast.4, ...), custom_call_target="tpu_custom_call" | custom-call | tf_op jit(solution)/shard_map/first_block/pallas_call | solution.py:268
  5.7 2.7 %collective-permute-start = (f16[264,128]{1,0:T(8,128)(2,1)S(1)}, f16[264,128]{1,0:T(8,128)(2,1)S(1)}, u32[]{:S(2)}, u32[]{:S(2)}) collective-permute-start(f16[264,128]{1,0:T(8,128)(2,1)S(1)} %multiply_convert_fusion.1), channel_id=1, source_target_pairs={{0,8},{4,12},{8,0},{12,4},{1,9},{5,13},{9,1},{13,5},{2,10},{6,14},... | collective-permute-start | bytes 202760 | tf_op jit(solution)/shard_map/ppermute | solution.py:298
  8.3 0.0 collective-permute-done.2.next_ref
  8.3 1.4 %last_block.1.last_ref = f32[256,128]{1,0:T(8,128)S(1)} custom-call(s32[2,32]{1,0:T(2,128)} %moves_hbm.3, s32[2,2]{1,0:T(2,128)} %flags_hbm.3, bf16[3,2,512]{2,1,0:T(2,128)(2,1)S(1)} %get-tuple-element.11.later_ref, bf16[3,2,2048]{2,1,0:T(2,128)(2,1)S(1)} %collective-permute-done.2.next_ref, bf16[2,32,1200]{2,1,0:T(8,128)(2,1)S(1)} %get-tuple-element.12.turned_ref, ...), custom_call_target="tpu_custom_call" | custom-call | tf_op jit(solution)/shard_map/last_block/pallas_call | solution.py:285
  9.7 1.4 %collective-permute-start.5 = (f16[256,128]{1,0:T(8,128)(2,1)S(1)}, f16[256,128]{1,0:T(8,128)(2,1)S(1)}, u32[]{:S(2)}, u32[]{:S(2)}) collective-permute-start(f16[256,128]{1,0:T(8,128)(2,1)S(1)} %multiply_convert_fusion.2), channel_id=1, source_target_pairs={{0,12},{4,8},{8,4},{12,0},{1,13},{5,9},{9,5},{13,1},{2,14},{6,10},... | collective-permute-start | bytes 196616 | tf_op jit(solution)/shard_map/ppermute | solution.py:298
  11.1 0.3 %collective-permute-start.4 = (f16[256,128]{1,0:T(8,128)(2,1)S(1)}, f16[256,128]{1,0:T(8,128)(2,1)S(1)}, u32[]{:S(2)}, u32[]{:S(2)}) collective-permute-start(f16[256,128]{1,0:T(8,128)(2,1)S(1)} %multiply_convert_fusion.2), channel_id=1, source_target_pairs={{0,4},{4,0},{8,12},{12,8},{1,5},{5,1},{9,13},{13,9},{2,6},{6,2},{1... | collective-permute-start | bytes 196616 | tf_op jit(solution)/shard_map/ppermute | solution.py:298
  11.4 2.7 %collective-permute-start.3 = (f16[256,128]{1,0:T(8,128)(2,1)S(1)}, f16[256,128]{1,0:T(8,128)(2,1)S(1)}, u32[]{:S(2)}, u32[]{:S(2)}) collective-permute-start(f16[256,128]{1,0:T(8,128)(2,1)S(1)} %multiply_convert_fusion.2), channel_id=1, source_target_pairs={{0,8},{4,12},{8,0},{12,4},{1,9},{5,13},{9,1},{13,5},{2,10},{6,14},... | collective-permute-start | bytes 196616 | tf_op jit(solution)/shard_map/ppermute | solution.py:298
  14.2 0.0 collective-permute-done
  14.2 0.8 %collective-permute-start.1 = (f16[264,128]{1,0:T(8,128)(2,1)S(1)}, f16[264,128]{1,0:T(8,128)(2,1)S(1)}, u32[]{:S(2)}, u32[]{:S(2)}) collective-permute-start(f16[264,128]{1,0:T(8,128)(2,1)S(1)} %get-tuple-element.15), channel_id=1, source_target_pairs={{0,4},{4,0},{8,12},{12,8},{1,5},{5,1},{9,13},{13,9},{2,6},{6,2},{1... | collective-permute-start | bytes 202760 | tf_op jit(solution)/shard_map/ppermute | solution.py:298
  15.0 1.7 %collective-permute-done.5 = f16[256,128]{1,0:T(8,128)(2,1)S(1)} collective-permute-done((f16[256,128]{1,0:T(8,128)(2,1)S(1)}, f16[256,128]{1,0:T(8,128)(2,1)S(1)}, u32[]{:S(2)}, u32[]{:S(2)}) %collective-permute-start.5) | collective-permute-done | bytes 65568 | tf_op jit(solution)/shard_map/ppermute | solution.py:298
  16.7 0.0 collective-permute-done.4
  16.7 1.1 %collective-permute-done.3 = f16[256,128]{1,0:T(8,128)(2,1)S(1)} collective-permute-done((f16[256,128]{1,0:T(8,128)(2,1)S(1)}, f16[256,128]{1,0:T(8,128)(2,1)S(1)}, u32[]{:S(2)}, u32[]{:S(2)}) %collective-permute-start.3) | collective-permute-done | bytes 65568 | tf_op jit(solution)/shard_map/ppermute | solution.py:298
  17.7 0.8 %collective-permute-done.1 = f16[264,128]{1,0:T(8,128)(2,1)S(1)} collective-permute-done((f16[264,128]{1,0:T(8,128)(2,1)S(1)}, f16[264,128]{1,0:T(8,128)(2,1)S(1)}, u32[]{:S(2)}, u32[]{:S(2)}) %collective-permute-start.1) | collective-permute-done | bytes 67616 | tf_op jit(solution)/shard_map/ppermute | solution.py:298
  18.6 0.9 %finish.1 = f32[32,2048]{1,0:T(8,128)} custom-call(f32[264,128]{1,0:T(8,128)S(1)} %get-tuple-element.16.first_ref, f32[264,128]{1,0:T(8,128)S(1)} %convert_multiply_fusion.near_ref, f32[256,128]{1,0:T(8,128)S(1)} %last_block.1.last_ref, f32[256,128]{1,0:T(8,128)S(1)} %add_multiply_fusion.far_ref), custom_call_target="tpu_custom_call" | custom-call | tf_op jit(solution)/shard_map/finish/pallas_call | solution.py:316
  (5 shorter events, 0.1 us)
Async XLA Ops:
  0.0 8.3 %collective-permute-start.2 = (bf16[3,2,2048]{2,1,0:T(2,128)(2,1)}, bf16[3,2,2048]{2,1,0:T(2,128)(2,1)S(1)}, u32[]{:S(2)}, u32[]{:S(2)}) collective-permute-start(bf16[3,2,2048]{2,1,0:T(2,128)(2,1)} %bitcast.3), channel_id=1, source_target_pairs={{0,2},{2,0},{1,3},{3,1},{4,6},{6,4},{5,7},{7,5},{8,10},{10,8},{9,1... | collective-permute-start | bytes 73736 | tf_op jit(solution)/shard_map/ppermute | solution.py:23
  5.7 8.5 %collective-permute-start = (f16[264,128]{1,0:T(8,128)(2,1)S(1)}, f16[264,128]{1,0:T(8,128)(2,1)S(1)}, u32[]{:S(2)}, u32[]{:S(2)}) collective-permute-start(f16[264,128]{1,0:T(8,128)(2,1)S(1)} %multiply_convert_fusion.1), channel_id=1, source_target_pairs={{0,8},{4,12},{8,0},{12,4},{1,9},{5,13},{9,1},{13,5},{2,10},{6,14},... | collective-permute-start | bytes 202760 | tf_op jit(solution)/shard_map/ppermute | solution.py:298
  9.7 6.9 %collective-permute-start.5 = (f16[256,128]{1,0:T(8,128)(2,1)S(1)}, f16[256,128]{1,0:T(8,128)(2,1)S(1)}, u32[]{:S(2)}, u32[]{:S(2)}) collective-permute-start(f16[256,128]{1,0:T(8,128)(2,1)S(1)} %multiply_convert_fusion.2), channel_id=1, source_target_pairs={{0,12},{4,8},{8,4},{12,0},{1,13},{5,9},{9,5},{13,1},{2,14},{6,10},... | collective-permute-start | bytes 196616 | tf_op jit(solution)/shard_map/ppermute | solution.py:298
  11.1 5.5 %collective-permute-start.4 = (f16[256,128]{1,0:T(8,128)(2,1)S(1)}, f16[256,128]{1,0:T(8,128)(2,1)S(1)}, u32[]{:S(2)}, u32[]{:S(2)}) collective-permute-start(f16[256,128]{1,0:T(8,128)(2,1)S(1)} %multiply_convert_fusion.2), channel_id=1, source_target_pairs={{0,4},{4,0},{8,12},{12,8},{1,5},{5,1},{9,13},{13,9},{2,6},{6,2},{1... | collective-permute-start | bytes 196616 | tf_op jit(solution)/shard_map/ppermute | solution.py:298
  11.4 6.3 %collective-permute-start.3 = (f16[256,128]{1,0:T(8,128)(2,1)S(1)}, f16[256,128]{1,0:T(8,128)(2,1)S(1)}, u32[]{:S(2)}, u32[]{:S(2)}) collective-permute-start(f16[256,128]{1,0:T(8,128)(2,1)S(1)} %multiply_convert_fusion.2), channel_id=1, source_target_pairs={{0,8},{4,12},{8,0},{12,4},{1,9},{5,13},{9,1},{13,5},{2,10},{6,14},... | collective-permute-start | bytes 196616 | tf_op jit(solution)/shard_map/ppermute | solution.py:298
  14.2 4.4 %collective-permute-start.1 = (f16[264,128]{1,0:T(8,128)(2,1)S(1)}, f16[264,128]{1,0:T(8,128)(2,1)S(1)}, u32[]{:S(2)}, u32[]{:S(2)}) collective-permute-start(f16[264,128]{1,0:T(8,128)(2,1)S(1)} %get-tuple-element.15), channel_id=1, source_target_pairs={{0,4},{4,0},{8,12},{12,8},{1,5},{5,1},{9,13},{13,9},{2,6},{6,2},{1... | collective-permute-start | bytes 202760 | tf_op jit(solution)/shard_map/ppermute | solution.py:298

commit v7 on v6

--- a/solution.py
+++ b/solution.py
@@ -14,7 +14,7 @@
 LANES = 128
 GROUP = 16
 COUNT_ROWS = 8
-TILES = 4
+TILES = 3
 WIRE_SCALE = 2.0**13
 
 

time: 19.6 us -> 19.7 us (level)
  no operation moved by 1% of the time
where the time goes in v7:
time: 19.7 us; the launch traced here: 19.5 us
  starting transfers between devices  10.8 us (55%)
  Pallas kernels  4.97 us (25%)
  waiting for transfers between devices  3.58 us (18%)
    ppermute x5, starting transfers between devices, exchange(): return lax.ppermute(part, 'sta', [(k, k ^ step) for k in range(number)])  7.86 us
    ppermute x5, waiting for transfers between devices, exchange(): return lax.ppermute(part, 'sta', [(k, k ^ step) for k in range(number)])  3.57 us
    ppermute x1, starting transfers between devices, from_next(): lax.ppermute(value, axis, [(k, (k - 1) % count) for k in range(count)])  2.94 us
    pallas_call x1, Pallas kernels, shards(): pl.pallas_call(first_block, out_shape=(jax.ShapeDtypeStruct((count * rows...  2.7 us
    pallas_call x1, Pallas kernels, shards(): pl.pallas_call(functools.partial(last_block, taps=taps), out_shape=jax.Sh...  1.41 us
    pallas_call x1, Pallas kernels, shards(): pl.pallas_call(functools.partial(finish, factor=math.sqrt(comps * taps)),...  0.87 us
  transfers between devices with their start and end apart: 6, of which 3 were waited for; matrix products, arithmetic and copies ran while one was open for 1% of the time, Pallas kernels for 21%

profile of v7, /device:TPU:0, one launch (start us, length us, event | category | flops | bytes accessed | tf_op | source)
XLA Modules:
  0.0 19.5 jit_solution(3892906552371279235)
XLA Ops:
  0.0 2.9 %collective-permute-start.2 = (bf16[3,2,2048]{2,1,0:T(2,128)(2,1)}, bf16[3,2,2048]{2,1,0:T(2,128)(2,1)S(1)}, u32[]{:S(2)}, u32[]{:S(2)}) collective-permute-start(bf16[3,2,2048]{2,1,0:T(2,128)(2,1)} %bitcast.3), channel_id=1, source_target_pairs={{0,2},{2,0},{1,3},{3,1},{4,6},{6,4},{5,7},{7,5},{8,10},{10,8},{9,1... | collective-permute-start | bytes 73736 | tf_op jit(solution)/shard_map/ppermute | solution.py:23
  2.9 2.7 %first_block.1 = (f32[264,128]{1,0:T(8,128)S(1)}, bf16[3,2,512]{2,1,0:T(2,128)(2,1)S(1)}, bf16[2,32,1200]{2,1,0:T(8,128)(2,1)S(1)}, f32[2,32,128]{2,1,0:T(8,128)S(1)}, f32[256,128]{1,0:T(8,128)S(1)}) custom-call(s32[2,32]{1,0:T(2,128)} %moves_hbm.3, s32[2,2]{1,0:T(2,128)} %flags_hbm.3, bf16[3,2,2048]{2,1,0:T(2,128)(2,1)} %bitcast.4, ...), custom_call_target="tpu_custom_call" | custom-call | tf_op jit(solution)/shard_map/first_block/pallas_call | solution.py:268
  5.7 2.7 %collective-permute-start = (f16[264,128]{1,0:T(8,128)(2,1)S(1)}, f16[264,128]{1,0:T(8,128)(2,1)S(1)}, u32[]{:S(2)}, u32[]{:S(2)}) collective-permute-start(f16[264,128]{1,0:T(8,128)(2,1)S(1)} %multiply_convert_fusion.1), channel_id=1, source_target_pairs={{0,8},{4,12},{8,0},{12,4},{1,9},{5,13},{9,1},{13,5},{2,10},{6,14},... | collective-permute-start | bytes 202760 | tf_op jit(solution)/shard_map/ppermute | solution.py:298
  8.3 0.0 collective-permute-done.2.next_ref
  8.3 1.4 %last_block.1.last_ref = f32[256,128]{1,0:T(8,128)S(1)} custom-call(s32[2,32]{1,0:T(2,128)} %moves_hbm.3, s32[2,2]{1,0:T(2,128)} %flags_hbm.3, bf16[3,2,512]{2,1,0:T(2,128)(2,1)S(1)} %get-tuple-element.11.later_ref, bf16[3,2,2048]{2,1,0:T(2,128)(2,1)S(1)} %collective-permute-done.2.next_ref, bf16[2,32,1200]{2,1,0:T(8,128)(2,1)S(1)} %get-tuple-element.12.turned_ref, ...), custom_call_target="tpu_custom_call" | custom-call | tf_op jit(solution)/shard_map/last_block/pallas_call | solution.py:285
  9.8 1.4 %collective-permute-start.5 = (f16[256,128]{1,0:T(8,128)(2,1)S(1)}, f16[256,128]{1,0:T(8,128)(2,1)S(1)}, u32[]{:S(2)}, u32[]{:S(2)}) collective-permute-start(f16[256,128]{1,0:T(8,128)(2,1)S(1)} %multiply_convert_fusion.2), channel_id=1, source_target_pairs={{0,12},{4,8},{8,4},{12,0},{1,13},{5,9},{9,5},{13,1},{2,14},{6,10},... | collective-permute-start | bytes 196616 | tf_op jit(solution)/shard_map/ppermute | solution.py:298
  11.2 0.3 %collective-permute-start.4 = (f16[256,128]{1,0:T(8,128)(2,1)S(1)}, f16[256,128]{1,0:T(8,128)(2,1)S(1)}, u32[]{:S(2)}, u32[]{:S(2)}) collective-permute-start(f16[256,128]{1,0:T(8,128)(2,1)S(1)} %multiply_convert_fusion.2), channel_id=1, source_target_pairs={{0,4},{4,0},{8,12},{12,8},{1,5},{5,1},{9,13},{13,9},{2,6},{6,2},{1... | collective-permute-start | bytes 196616 | tf_op jit(solution)/shard_map/ppermute | solution.py:298
  11.5 2.7 %collective-permute-start.3 = (f16[256,128]{1,0:T(8,128)(2,1)S(1)}, f16[256,128]{1,0:T(8,128)(2,1)S(1)}, u32[]{:S(2)}, u32[]{:S(2)}) collective-permute-start(f16[256,128]{1,0:T(8,128)(2,1)S(1)} %multiply_convert_fusion.2), channel_id=1, source_target_pairs={{0,8},{4,12},{8,0},{12,4},{1,9},{5,13},{9,1},{13,5},{2,10},{6,14},... | collective-permute-start | bytes 196616 | tf_op jit(solution)/shard_map/ppermute | solution.py:298
  14.2 0.0 collective-permute-done
  14.3 0.8 %collective-permute-start.1 = (f16[264,128]{1,0:T(8,128)(2,1)S(1)}, f16[264,128]{1,0:T(8,128)(2,1)S(1)}, u32[]{:S(2)}, u32[]{:S(2)}) collective-permute-start(f16[264,128]{1,0:T(8,128)(2,1)S(1)} %get-tuple-element.15), channel_id=1, source_target_pairs={{0,4},{4,0},{8,12},{12,8},{1,5},{5,1},{9,13},{13,9},{2,6},{6,2},{1... | collective-permute-start | bytes 202760 | tf_op jit(solution)/shard_map/ppermute | solution.py:298
  15.0 1.7 %collective-permute-done.5 = f16[256,128]{1,0:T(8,128)(2,1)S(1)} collective-permute-done((f16[256,128]{1,0:T(8,128)(2,1)S(1)}, f16[256,128]{1,0:T(8,128)(2,1)S(1)}, u32[]{:S(2)}, u32[]{:S(2)}) %collective-permute-start.5) | collective-permute-done | bytes 65568 | tf_op jit(solution)/shard_map/ppermute | solution.py:298
  16.7 0.0 collective-permute-done.4
  16.7 1.1 %collective-permute-done.3 = f16[256,128]{1,0:T(8,128)(2,1)S(1)} collective-permute-done((f16[256,128]{1,0:T(8,128)(2,1)S(1)}, f16[256,128]{1,0:T(8,128)(2,1)S(1)}, u32[]{:S(2)}, u32[]{:S(2)}) %collective-permute-start.3) | collective-permute-done | bytes 65568 | tf_op jit(solution)/shard_map/ppermute | solution.py:298
  17.8 0.8 %collective-permute-done.1 = f16[264,128]{1,0:T(8,128)(2,1)S(1)} collective-permute-done((f16[264,128]{1,0:T(8,128)(2,1)S(1)}, f16[264,128]{1,0:T(8,128)(2,1)S(1)}, u32[]{:S(2)}, u32[]{:S(2)}) %collective-permute-start.1) | collective-permute-done | bytes 67616 | tf_op jit(solution)/shard_map/ppermute | solution.py:298
  18.6 0.9 %finish.1 = f32[32,2048]{1,0:T(8,128)} custom-call(f32[264,128]{1,0:T(8,128)S(1)} %get-tuple-element.16.first_ref, f32[264,128]{1,0:T(8,128)S(1)} %convert_multiply_fusion.near_ref, f32[256,128]{1,0:T(8,128)S(1)} %last_block.1.last_ref, f32[256,128]{1,0:T(8,128)S(1)} %add_multiply_fusion.far_ref), custom_call_target="tpu_custom_call" | custom-call | tf_op jit(solution)/shard_map/finish/pallas_call | solution.py:316
  (5 shorter events, 0.1 us)
Async XLA Ops:
  0.0 8.3 %collective-permute-start.2 = (bf16[3,2,2048]{2,1,0:T(2,128)(2,1)}, bf16[3,2,2048]{2,1,0:T(2,128)(2,1)S(1)}, u32[]{:S(2)}, u32[]{:S(2)}) collective-permute-start(bf16[3,2,2048]{2,1,0:T(2,128)(2,1)} %bitcast.3), channel_id=1, source_target_pairs={{0,2},{2,0},{1,3},{3,1},{4,6},{6,4},{5,7},{7,5},{8,10},{10,8},{9,1... | collective-permute-start | bytes 73736 | tf_op jit(solution)/shard_map/ppermute | solution.py:23
  5.7 8.6 %collective-permute-start = (f16[264,128]{1,0:T(8,128)(2,1)S(1)}, f16[264,128]{1,0:T(8,128)(2,1)S(1)}, u32[]{:S(2)}, u32[]{:S(2)}) collective-permute-start(f16[264,128]{1,0:T(8,128)(2,1)S(1)} %multiply_convert_fusion.1), channel_id=1, source_target_pairs={{0,8},{4,12},{8,0},{12,4},{1,9},{5,13},{9,1},{13,5},{2,10},{6,14},... | collective-permute-start | bytes 202760 | tf_op jit(solution)/shard_map/ppermute | solution.py:298
  9.8 6.9 %collective-permute-start.5 = (f16[256,128]{1,0:T(8,128)(2,1)S(1)}, f16[256,128]{1,0:T(8,128)(2,1)S(1)}, u32[]{:S(2)}, u32[]{:S(2)}) collective-permute-start(f16[256,128]{1,0:T(8,128)(2,1)S(1)} %multiply_convert_fusion.2), channel_id=1, source_target_pairs={{0,12},{4,8},{8,4},{12,0},{1,13},{5,9},{9,5},{13,1},{2,14},{6,10},... | collective-permute-start | bytes 196616 | tf_op jit(solution)/shard_map/ppermute | solution.py:298
  11.2 5.5 %collective-permute-start.4 = (f16[256,128]{1,0:T(8,128)(2,1)S(1)}, f16[256,128]{1,0:T(8,128)(2,1)S(1)}, u32[]{:S(2)}, u32[]{:S(2)}) collective-permute-start(f16[256,128]{1,0:T(8,128)(2,1)S(1)} %multiply_convert_fusion.2), channel_id=1, source_target_pairs={{0,4},{4,0},{8,12},{12,8},{1,5},{5,1},{9,13},{13,9},{2,6},{6,2},{1... | collective-permute-start | bytes 196616 | tf_op jit(solution)/shard_map/ppermute | solution.py:298
  11.5 6.3 %collective-permute-start.3 = (f16[256,128]{1,0:T(8,128)(2,1)S(1)}, f16[256,128]{1,0:T(8,128)(2,1)S(1)}, u32[]{:S(2)}, u32[]{:S(2)}) collective-permute-start(f16[256,128]{1,0:T(8,128)(2,1)S(1)} %multiply_convert_fusion.2), channel_id=1, source_target_pairs={{0,8},{4,12},{8,0},{12,4},{1,9},{5,13},{9,1},{13,5},{2,10},{6,14},... | collective-permute-start | bytes 196616 | tf_op jit(solution)/shard_map/ppermute | solution.py:298
  14.3 4.4 %collective-permute-start.1 = (f16[264,128]{1,0:T(8,128)(2,1)S(1)}, f16[264,128]{1,0:T(8,128)(2,1)S(1)}, u32[]{:S(2)}, u32[]{:S(2)}) collective-permute-start(f16[264,128]{1,0:T(8,128)(2,1)S(1)} %get-tuple-element.15), channel_id=1, source_target_pairs={{0,4},{4,0},{8,12},{12,8},{1,5},{5,1},{9,13},{13,9},{2,6},{6,2},{1... | collective-permute-start | bytes 202760 | tf_op jit(solution)/shard_map/ppermute | solution.py:298

commit v8 on v6

--- a/solution.py
+++ b/solution.py
@@ -297,6 +297,9 @@
     def exchange(part, step):
         return lax.ppermute(part, "sta", [(k, k ^ step) for k in range(number)])
 
+    def around(part, step):
+        return lax.ppermute(part, "sta", [(k, (k + step) % number) for k in range(number)])
+
     def code(part):
         return (part * WIRE_SCALE).astype(jnp.float16)
 
@@ -306,7 +309,7 @@
     if number == 4:
         far_first = exchange(code(first), 2)
         coded_last = code(last)
-        far = [exchange(coded_last, step) for step in (2, 1, 3)]
+        far = [around(coded_last, step) for step in (3, 1, 2)]
         first = first + decode(far_first)
         near = decode(exchange(code(first), 1))
         far = decode(far[0]) + decode(far[1]) + decode(far[2])

time: 19.6 us -> 19.7 us (level)
  waiting for transfers between devices: 3.57 us -> 4.17 us
  starting transfers between devices: 10.8 us -> 10.3 us
    ppermute x5 -> x2, starting transfers between devices: 7.86 us -> 3.08 us  [exchange(): return lax.ppermute(part, 'sta', [(k, k ^ step) for k in range(number)])]
    ppermute x0 -> x3, starting transfers between devices: none -> 4.23 us  [around(): lax.ppermute(part, 'sta', [(k, (k + step) % number) for k in range(number)])]
    ppermute x0 -> x3, waiting for transfers between devices: none -> 3.47 us  [around(): lax.ppermute(part, 'sta', [(k, (k + step) % number) for k in range(number)])]
    ppermute x5 -> x2, waiting for transfers between devices: 3.57 us -> 0.69 us  [exchange(): return lax.ppermute(part, 'sta', [(k, k ^ step) for k in range(number)])]
where the time goes in v8:
time: 19.7 us; the launch traced here: 19.5 us
  starting transfers between devices  10.3 us (52%)
  Pallas kernels  4.92 us (25%)
  waiting for transfers between devices  4.17 us (21%)
    ppermute x3, starting transfers between devices, around(): lax.ppermute(part, 'sta', [(k, (k + step) % number) for k in range(number)])  4.23 us
    ppermute x3, waiting for transfers between devices, around(): lax.ppermute(part, 'sta', [(k, (k + step) % number) for k in range(number)])  3.47 us
    ppermute x2, starting transfers between devices, exchange(): return lax.ppermute(part, 'sta', [(k, k ^ step) for k in range(number)])  3.08 us
    ppermute x1, starting transfers between devices, from_next(): lax.ppermute(value, axis, [(k, (k - 1) % count) for k in range(count)])  2.94 us
    pallas_call x1, Pallas kernels, shards(): pl.pallas_call(first_block, out_shape=(jax.ShapeDtypeStruct((count * rows...  2.69 us
    pallas_call x1, Pallas kernels, shards(): pl.pallas_call(functools.partial(last_block, taps=taps), out_shape=jax.Sh...  1.36 us
    pallas_call x1, Pallas kernels, shards(): pl.pallas_call(functools.partial(finish, factor=math.sqrt(comps * taps)),...  0.87 us
    ppermute x2, waiting for transfers between devices, exchange(): return lax.ppermute(part, 'sta', [(k, k ^ step) for k in range(number)])  0.69 us
  transfers between devices with their start and end apart: 6, of which 3 were waited for; matrix products, arithmetic and copies ran while one was open for 1% of the time, Pallas kernels for 21%

profile of v8, /device:TPU:0, one launch (start us, length us, event | category | flops | bytes accessed | tf_op | source)
XLA Modules:
  0.0 19.5 jit_solution(16183937822963383568)
XLA Ops:
  0.0 2.9 %collective-permute-start.2 = (bf16[3,2,2048]{2,1,0:T(2,128)(2,1)}, bf16[3,2,2048]{2,1,0:T(2,128)(2,1)S(1)}, u32[]{:S(2)}, u32[]{:S(2)}) collective-permute-start(bf16[3,2,2048]{2,1,0:T(2,128)(2,1)} %bitcast.3), channel_id=1, source_target_pairs={{0,2},{2,0},{1,3},{3,1},{4,6},{6,4},{5,7},{7,5},{8,10},{10,8},{9,1... | collective-permute-start | bytes 73736 | tf_op jit(solution)/shard_map/ppermute | solution.py:23
  2.9 2.7 %first_block.1 = (f32[264,128]{1,0:T(8,128)S(1)}, bf16[3,2,512]{2,1,0:T(2,128)(2,1)S(1)}, bf16[2,32,1200]{2,1,0:T(8,128)(2,1)S(1)}, f32[2,32,128]{2,1,0:T(8,128)S(1)}, f32[256,128]{1,0:T(8,128)S(1)}) custom-call(s32[2,32]{1,0:T(2,128)} %moves_hbm.3, s32[2,2]{1,0:T(2,128)} %flags_hbm.3, bf16[3,2,2048]{2,1,0:T(2,128)(2,1)} %bitcast.4, ...), custom_call_target="tpu_custom_call" | custom-call | tf_op jit(solution)/shard_map/first_block/pallas_call | solution.py:268
  5.7 2.7 %collective-permute-start = (f16[264,128]{1,0:T(8,128)(2,1)S(1)}, f16[264,128]{1,0:T(8,128)(2,1)S(1)}, u32[]{:S(2)}, u32[]{:S(2)}) collective-permute-start(f16[264,128]{1,0:T(8,128)(2,1)S(1)} %multiply_convert_fusion.1), channel_id=1, source_target_pairs={{0,8},{4,12},{8,0},{12,4},{1,9},{5,13},{9,1},{13,5},{2,10},{6,14},... | collective-permute-start | bytes 202760 | tf_op jit(solution)/shard_map/ppermute | solution.py:298
  8.3 0.0 collective-permute-done.2.next_ref
  8.3 1.4 %last_block.1.last_ref = f32[256,128]{1,0:T(8,128)S(1)} custom-call(s32[2,32]{1,0:T(2,128)} %moves_hbm.3, s32[2,2]{1,0:T(2,128)} %flags_hbm.3, bf16[3,2,512]{2,1,0:T(2,128)(2,1)S(1)} %get-tuple-element.11.later_ref, bf16[3,2,2048]{2,1,0:T(2,128)(2,1)S(1)} %collective-permute-done.2.next_ref, bf16[2,32,1200]{2,1,0:T(8,128)(2,1)S(1)} %get-tuple-element.12.turned_ref, ...), custom_call_target="tpu_custom_call" | custom-call | tf_op jit(solution)/shard_map/last_block/pallas_call | solution.py:285
  9.7 0.4 %collective-permute-start.5 = (f16[256,128]{1,0:T(8,128)(2,1)S(1)}, f16[256,128]{1,0:T(8,128)(2,1)S(1)}, u32[]{:S(2)}, u32[]{:S(2)}) collective-permute-start(f16[256,128]{1,0:T(8,128)(2,1)S(1)} %multiply_convert_fusion.2), channel_id=1, source_target_pairs={{0,8},{4,12},{8,0},{12,4},{1,9},{5,13},{9,1},{13,5},{2,10},{6,14},... | collective-permute-start | bytes 196616 | tf_op jit(solution)/shard_map/ppermute | solution.py:301
  10.1 1.6 %collective-permute-start.4 = (f16[256,128]{1,0:T(8,128)(2,1)S(1)}, f16[256,128]{1,0:T(8,128)(2,1)S(1)}, u32[]{:S(2)}, u32[]{:S(2)}) collective-permute-start(f16[256,128]{1,0:T(8,128)(2,1)S(1)} %multiply_convert_fusion.2), channel_id=1, source_target_pairs={{0,4},{4,8},{8,12},{12,0},{1,5},{5,9},{9,13},{13,1},{2,6},{6,10},{... | collective-permute-start | bytes 196616 | tf_op jit(solution)/shard_map/ppermute | solution.py:301
  11.7 2.2 %collective-permute-start.3 = (f16[256,128]{1,0:T(8,128)(2,1)S(1)}, f16[256,128]{1,0:T(8,128)(2,1)S(1)}, u32[]{:S(2)}, u32[]{:S(2)}) collective-permute-start(f16[256,128]{1,0:T(8,128)(2,1)S(1)} %multiply_convert_fusion.2), channel_id=1, source_target_pairs={{0,12},{4,0},{8,4},{12,8},{1,13},{5,1},{9,5},{13,9},{2,14},{6,2},{... | collective-permute-start | bytes 196616 | tf_op jit(solution)/shard_map/ppermute | solution.py:301
  13.9 0.0 collective-permute-done
  14.0 0.4 %collective-permute-start.1 = (f16[264,128]{1,0:T(8,128)(2,1)S(1)}, f16[264,128]{1,0:T(8,128)(2,1)S(1)}, u32[]{:S(2)}, u32[]{:S(2)}) collective-permute-start(f16[264,128]{1,0:T(8,128)(2,1)S(1)} %get-tuple-element.15), channel_id=1, source_target_pairs={{0,4},{4,0},{8,12},{12,8},{1,5},{5,1},{9,13},{13,9},{2,6},{6,2},{1... | collective-permute-start | bytes 202760 | tf_op jit(solution)/shard_map/ppermute | solution.py:298
  14.4 3.1 %collective-permute-done.5 = f16[256,128]{1,0:T(8,128)(2,1)S(1)} collective-permute-done((f16[256,128]{1,0:T(8,128)(2,1)S(1)}, f16[256,128]{1,0:T(8,128)(2,1)S(1)}, u32[]{:S(2)}, u32[]{:S(2)}) %collective-permute-start.5) | collective-permute-done | bytes 65568 | tf_op jit(solution)/shard_map/ppermute | solution.py:301
  17.5 0.4 %collective-permute-done.4 = f16[256,128]{1,0:T(8,128)(2,1)S(1)} collective-permute-done((f16[256,128]{1,0:T(8,128)(2,1)S(1)}, f16[256,128]{1,0:T(8,128)(2,1)S(1)}, u32[]{:S(2)}, u32[]{:S(2)}) %collective-permute-start.4) | collective-permute-done | bytes 65568 | tf_op jit(solution)/shard_map/ppermute | solution.py:301
  17.9 0.0 collective-permute-done.3
  17.9 0.7 %collective-permute-done.1 = f16[264,128]{1,0:T(8,128)(2,1)S(1)} collective-permute-done((f16[264,128]{1,0:T(8,128)(2,1)S(1)}, f16[264,128]{1,0:T(8,128)(2,1)S(1)}, u32[]{:S(2)}, u32[]{:S(2)}) %collective-permute-start.1) | collective-permute-done | bytes 67616 | tf_op jit(solution)/shard_map/ppermute | solution.py:298
  18.6 0.9 %finish.1 = f32[32,2048]{1,0:T(8,128)} custom-call(f32[264,128]{1,0:T(8,128)S(1)} %get-tuple-element.16.first_ref, f32[264,128]{1,0:T(8,128)S(1)} %convert_multiply_fusion.near_ref, f32[256,128]{1,0:T(8,128)S(1)} %last_block.1.last_ref, f32[256,128]{1,0:T(8,128)S(1)} %add_multiply_fusion.far_ref), custom_call_target="tpu_custom_call" | custom-call | tf_op jit(solution)/shard_map/finish/pallas_call | solution.py:319
  (5 shorter events, 0.1 us)
Async XLA Ops:
  0.0 8.3 %collective-permute-start.2 = (bf16[3,2,2048]{2,1,0:T(2,128)(2,1)}, bf16[3,2,2048]{2,1,0:T(2,128)(2,1)S(1)}, u32[]{:S(2)}, u32[]{:S(2)}) collective-permute-start(bf16[3,2,2048]{2,1,0:T(2,128)(2,1)} %bitcast.3), channel_id=1, source_target_pairs={{0,2},{2,0},{1,3},{3,1},{4,6},{6,4},{5,7},{7,5},{8,10},{10,8},{9,1... | collective-permute-start | bytes 73736 | tf_op jit(solution)/shard_map/ppermute | solution.py:23
  5.7 8.3 %collective-permute-start = (f16[264,128]{1,0:T(8,128)(2,1)S(1)}, f16[264,128]{1,0:T(8,128)(2,1)S(1)}, u32[]{:S(2)}, u32[]{:S(2)}) collective-permute-start(f16[264,128]{1,0:T(8,128)(2,1)S(1)} %multiply_convert_fusion.1), channel_id=1, source_target_pairs={{0,8},{4,12},{8,0},{12,4},{1,9},{5,13},{9,1},{13,5},{2,10},{6,14},... | collective-permute-start | bytes 202760 | tf_op jit(solution)/shard_map/ppermute | solution.py:298
  9.7 7.8 %collective-permute-start.5 = (f16[256,128]{1,0:T(8,128)(2,1)S(1)}, f16[256,128]{1,0:T(8,128)(2,1)S(1)}, u32[]{:S(2)}, u32[]{:S(2)}) collective-permute-start(f16[256,128]{1,0:T(8,128)(2,1)S(1)} %multiply_convert_fusion.2), channel_id=1, source_target_pairs={{0,8},{4,12},{8,0},{12,4},{1,9},{5,13},{9,1},{13,5},{2,10},{6,14},... | collective-permute-start | bytes 196616 | tf_op jit(solution)/shard_map/ppermute | solution.py:301
  10.1 7.8 %collective-permute-start.4 = (f16[256,128]{1,0:T(8,128)(2,1)S(1)}, f16[256,128]{1,0:T(8,128)(2,1)S(1)}, u32[]{:S(2)}, u32[]{:S(2)}) collective-permute-start(f16[256,128]{1,0:T(8,128)(2,1)S(1)} %multiply_convert_fusion.2), channel_id=1, source_target_pairs={{0,4},{4,8},{8,12},{12,0},{1,5},{5,9},{9,13},{13,1},{2,6},{6,10},{... | collective-permute-start | bytes 196616 | tf_op jit(solution)/shard_map/ppermute | solution.py:301
  11.7 6.2 %collective-permute-start.3 = (f16[256,128]{1,0:T(8,128)(2,1)S(1)}, f16[256,128]{1,0:T(8,128)(2,1)S(1)}, u32[]{:S(2)}, u32[]{:S(2)}) collective-permute-start(f16[256,128]{1,0:T(8,128)(2,1)S(1)} %multiply_convert_fusion.2), channel_id=1, source_target_pairs={{0,12},{4,0},{8,4},{12,8},{1,13},{5,1},{9,5},{13,9},{2,14},{6,2},{... | collective-permute-start | bytes 196616 | tf_op jit(solution)/shard_map/ppermute | solution.py:301
  14.0 4.6 %collective-permute-start.1 = (f16[264,128]{1,0:T(8,128)(2,1)S(1)}, f16[264,128]{1,0:T(8,128)(2,1)S(1)}, u32[]{:S(2)}, u32[]{:S(2)}) collective-permute-start(f16[264,128]{1,0:T(8,128)(2,1)S(1)} %get-tuple-element.15), channel_id=1, source_target_pairs={{0,4},{4,0},{8,12},{12,8},{1,5},{5,1},{9,13},{13,9},{2,6},{6,2},{1... | collective-permute-start | bytes 202760 | tf_op jit(solution)/shard_map/ppermute | solution.py:298
